TPU v7x, 256 devices: a whole 4x4x8 slice. The times are simulated.
256 devices in a mesh: seq: 64 (over x, z, core), head: 4 (over y).
Axes of the slice: x: 4, y: 4, z: 8, core: 2. Of those that a mesh axis runs over, the one named last changes fastest.
Arguments:
- query_rows: bfloat16 [32768, 2048], P('seq', 'head'), may hold values from -6 to 6
- key_rows: bfloat16 [32768, 2048], P('seq', 'head'), may hold values from -6 to 6
- value_rows: bfloat16 [32768, 4096], P('seq', 'head'), may hold values from -6 to 6
- out_grad: bfloat16 [32768, 3072], P('seq', 'head'), may hold values from -6 to 6
- out_weight: bfloat16 [4096, 3072], P('head'), may hold values from -0.109375 to 0.109375
- level_codes: int32 [12, 32, 32768], P(None, 'head', 'seq'), may hold values from 0 to 15
- level_table: float32 [32, 16], P('head'), may hold values from 0.1 to 1
Outputs:
- query_grad: bfloat16 [32768, 2048], P('seq', 'head')
- key_grad: bfloat16 [32768, 2048], P('seq', 'head')
- value_grad: bfloat16 [32768, 4096], P('seq', 'head')
All inputs are finite; a program needn't handle non-finite values.
Results may differ from a plain program's by a relative error of at most 0.0062.
Values may be sent and summed in bfloat16 or wider, within the bound.
A program may use at most 128 MiB of HBM per device.

v0:
```python
import jax
import jax.numpy as jnp
from jax import lax
from jax.sharding import PartitionSpec as P

DK = 64
BLK = 64
LEVELS = 12


def swapped(x, axis, stride):
    return lax.ppermute(x, axis, [(i, i ^ 1 << stride) for i in range(lax.axis_size(axis))])


def level_scales():
    span_list = [DK * BLK * 2 ** max(level - 1, 0) for level in range(LEVELS)]
    return jnp.asarray([span ** (-0.5) for span in span_list], dtype=jnp.float32)


def level_weights(level_codes, level_table):
    entries = level_table.shape[1]
    picks = (level_codes[None] == jnp.arange(entries, dtype=jnp.int32)[:, None, None, None]).astype(
        jnp.float32
    )
    looked = jnp.einsum("jlht,hj->lht", picks, level_table, precision=lax.Precision.HIGHEST)
    return looked * level_scales()[:, None, None]


def per_device(query_rows, key_rows, value_rows, out_grad, out_weight, level_codes, level_table):
    heads = level_table.shape[0]
    row_count = query_rows.shape[0]
    query = query_rows.reshape(row_count, heads, -1)
    key_product = key_rows.reshape(row_count, heads, -1)
    value_product = value_rows.reshape(row_count, heads, -1)
    value_size = value_product.shape[2]
    weights = level_weights(level_codes, level_table)
    gathered = lax.dot_general(
        lax.all_gather(out_grad, "head", axis=1, tiled=True),
        out_weight,
        (((1,), (1,)), ((), ())),
        preferred_element_type=jnp.float32,
    )
    dgrad = gathered.astype(jnp.bfloat16).reshape(row_count, heads, value_size)
    low_bits = (row_count // BLK).bit_length() - 1
    places = jnp.arange(row_count, dtype=jnp.int32)
    block_id = places // BLK
    crossed = jnp.bitwise_xor(block_id[:, None], block_id[None, :])
    depth_map = jnp.zeros((row_count, row_count), jnp.int32)
    for exponent in range(low_bits):
        depth_map = depth_map + (crossed >= 2**exponent).astype(jnp.int32)
    causal = places[:, None] >= places[None, :]
    mixing = jnp.zeros((heads, row_count, row_count), jnp.float32)
    for level in range(low_bits + 1):
        chosen = jnp.logical_and(depth_map == level, causal)
        mixing = mixing + jnp.where(
            chosen[None], weights[level][:, :, None], jnp.zeros((), jnp.float32)
        )
    scores = jnp.einsum("thk,shk->hts", query, key_product, preferred_element_type=jnp.float32)
    grads = jnp.einsum("thv,shv->hts", dgrad, value_product, preferred_element_type=jnp.float32)
    grad_mix = (mixing * grads).astype(jnp.bfloat16)
    score_mix = (mixing * scores).astype(jnp.bfloat16)
    query_local = jnp.einsum(
        "hts,shk->thk", grad_mix, key_product, preferred_element_type=jnp.float32
    )
    key_local = jnp.einsum("hts,thk->shk", grad_mix, query, preferred_element_type=jnp.float32)
    value_local = jnp.einsum("hts,thv->shv", score_mix, dgrad, preferred_element_type=jnp.float32)
    seq_bits = lax.axis_size("seq").bit_length() - 1
    device = lax.axis_index("seq")
    local_level_state = jnp.einsum(
        "qrg,qri->rgi", key_product, value_product, preferred_element_type=jnp.float32
    )
    piece = lax.all_gather(local_level_state[None], "seq", axis=0, tiled=True)
    count = piece.shape[0]
    others = jnp.arange(count, dtype=jnp.int32)
    differ = jnp.bitwise_xor(device, others)
    below = others < device
    span_list = 2 ** jnp.arange(seq_bits, dtype=jnp.int32)
    inside = jnp.logical_and(
        differ[:, None] >= span_list[None, :], differ[:, None] < 2 * span_list[None, :]
    )
    member = jnp.logical_and(below[:, None], inside).astype(jnp.float32)
    states = jnp.einsum("nb,nhkv->bhkv", member, piece, precision=lax.Precision.HIGHEST)
    remote_weights = weights[low_bits + 1 : low_bits + 1 + seq_bits].transpose(0, 2, 1)
    bit_ids = jnp.arange(seq_bits, dtype=jnp.int32)
    upper_bits = jnp.bitwise_and(jnp.right_shift(device, bit_ids), 1).astype(jnp.float32)
    state_low = states.astype(jnp.bfloat16)
    readout = jnp.einsum("thv,bhkv->bthk", dgrad, state_low, preferred_element_type=jnp.float32)
    query_remote = jnp.sum(readout * remote_weights[..., None], axis=0)
    factor = (remote_weights * upper_bits[:, None, None])[..., None]
    scaled_query = (factor * query[None]).astype(jnp.bfloat16)
    level_grad = jnp.einsum(
        "bthk,thv->bhkv", scaled_query, dgrad, preferred_element_type=jnp.float32
    )
    remaining = level_grad
    returned = jnp.zeros(local_level_state.shape, jnp.float32)
    for bit_pos in range(seq_bits):
        partner = swapped(remaining, "seq", bit_pos)
        lower = jnp.bitwise_and(jnp.right_shift(device, bit_pos), 1) == 0
        returned = returned + jnp.where(lower, partner[0], jnp.zeros((), jnp.float32))
        remaining = (remaining + partner)[1:]
    returned_lower_part = returned.astype(jnp.bfloat16)
    key_remote = jnp.einsum(
        "sjb,job->sjo", value_product, returned_lower_part, preferred_element_type=jnp.float32
    )
    value_remote = jnp.einsum(
        "fnc,ncd->fnd", key_product, returned_lower_part, preferred_element_type=jnp.float32
    )
    query_grad = (query_local + query_remote).astype(jnp.bfloat16).reshape(row_count, -1)
    key_grad = (key_local + key_remote).astype(jnp.bfloat16).reshape(row_count, -1)
    value_grad = (value_local + value_remote).astype(jnp.bfloat16).reshape(row_count, -1)
    return (query_grad, key_grad, value_grad)


def solution(mesh):
    return jax.shard_map(
        per_device,
        mesh=mesh,
        in_specs=(
            P("seq", "head"),
            P("seq", "head"),
            P("seq", "head"),
            P("seq", "head"),
            P("head", None),
            P(None, "head", "seq"),
            P("head", None),
        ),
        out_specs=(P("seq", "head"), P("seq", "head"), P("seq", "head")),
        check_vma=False,
    )
```

profile of v0, /device:TPU:56, one launch (start us, length us, event | category | flops | bytes accessed | tf_op | source)
XLA Modules:
  0.0 298.3 jit_solution(3030046605879231683)
XLA Ops:
  11.2 2.6 fusion.10
  14.0 2.7 multiply_convert_fusion.2
  16.7 35.9 %all-gather.4.cloned.1.call-done = bf16[512,3072]{1,0:T(8,128)(2,1)} async-done(((bf16[512,768]{1,0:T(8,128)(2,1)}), bf16[512,3072]{1,0:T(8,128)(2,1)}) %all-gather.4.cloned.1.call-update) | async-done | bytes 3145744 | tf_op jit(solution)/shard_map/all_gather | solution.py:38
  52.6 7.2 %fusion.15 = bf16[64,8,8,128]{3,1,2,0:T(8,128)(2,1)S(1)} fusion(bf16[512,3072]{1,0:T(8,128)(2,1)} %all-gather.4.cloned.1.call-done, bf16[1024,3072]{1,0:T(8,128)(2,1)} %param.12), kind=kOutput, calls=%fused_computation.23 | convolution fusion | flops 3221749760 | bytes 10485760 | tf_op jit(solution)/shard_map/dot_general | solution.py:37
  61.5 3.1 %fusion.61 = f32[8,128,384]{1,2,0:S(1)} fusion(bf16[8,512,384]{1,2,0:T(8,128)(2,1)} %bitcast.101, bf16[512,8,128]{0,2,1:T(8,128)(2,1)} %copy.69), kind=kOutput, calls=%fused_computation.107 | convolution fusion | flops 402653184 | bytes 5767168
  64.7 3.4 %collective-permute-done = f32[6,8,64,128]{3,2,0,1:T(8,128)S(1)} collective-permute-done((f32[6,8,64,128]{3,2,0,1:T(8,128)S(1)}, f32[6,8,64,128]{3,2,0,1:T(8,128)S(1)}, u32[]{:S(2)}, u32[]{:S(2)}) %collective-permute-start) | collective-permute-done | bytes 1572896 | tf_op jit(solution)/shard_map/ppermute | solution.py:12
  68.8 40.3 %collective-permute-done.1 = f32[5,8,64,128]{3,2,0,1:T(8,128)S(1)} collective-permute-done((f32[5,8,64,128]{3,2,0,1:T(8,128)S(1)}, f32[5,8,64,128]{3,2,0,1:T(8,128)S(1)}, u32[]{:S(2)}, u32[]{:S(2)}) %collective-permute-start.1) | collective-permute-done | bytes 1310752 | tf_op jit(solution)/shard_map/ppermute | solution.py:12
  110.4 2.5 collective-permute-start.2
  114.2 66.6 %collective-permute-done.2 = f32[4,8,64,128]{3,2,0,1:T(8,128)} collective-permute-done((f32[4,8,64,128]{3,2,0,1:T(8,128)}, f32[4,8,64,128]{3,2,0,1:T(8,128)}, u32[]{:S(2)}, u32[]{:S(2)}) %collective-permute-start.2) | collective-permute-done | bytes 1048608 | tf_op jit(solution)/shard_map/ppermute | solution.py:12
  180.8 1.5 slice_add_fusion.2
  182.3 3.5 %collective-permute-start.3 = (f32[3,8,64,128]{3,2,0,1:T(8,128)S(1)}, f32[3,8,64,128]{3,2,0,1:T(8,128)S(1)}, u32[]{:S(2)}, u32[]{:S(2)}) collective-permute-start(f32[3,8,64,128]{3,2,0,1:T(8,128)S(1)} %slice_add_fusion.2), channel_id=1, source_target_pairs={{0,32},{4,36},{8,40},{12,44},{16,48},{20,52},{24,56},{28,60},{32,0... | collective-permute-start | bytes 2359304 | tf_op jit(solution)/shard_map/ppermute | solution.py:12
  187.0 1.7 fusion.28
  188.6 41.2 %collective-permute-done.3 = f32[3,8,64,128]{3,2,0,1:T(8,128)S(1)} collective-permute-done((f32[3,8,64,128]{3,2,0,1:T(8,128)S(1)}, f32[3,8,64,128]{3,2,0,1:T(8,128)S(1)}, u32[]{:S(2)}, u32[]{:S(2)}) %collective-permute-start.3) | collective-permute-done | bytes 786464 | tf_op jit(solution)/shard_map/ppermute | solution.py:12
  230.9 1.5 collective-permute-start.4
  232.3 7.5 %fusion.3 = f32[8,128,512]{2,1,0:T(8,128)} fusion(bf16[512,8,128]{0,2,1:T(8,128)(2,1)} %copy.69, f32[8,512]{1,0:T(8,128)} %get-tuple-element.16, f32[8,512]{1,0:T(8,128)} %get-tuple-element.17, f32[8,512]{1,0:T(8,128)} %get-tuple-element.18, f32[8,512]{1,0:T(8,128)S(1)} %get-tuple-element.15, pred[512,512]{1,0:T(8,128)(4,1)} %get-tuple-element.20, ...), kind=kOutput, calls=%fused_computation.8 | convolution fusion | flops 824180736 | bytes 5308416 | tf_op jit(solution)/shard_map/hts,thv->shv/dot_general | solution.py:66
  239.9 4.8 %collective-permute-done.4 = f32[2,8,64,128]{3,2,0,1:T(8,128)} collective-permute-done((f32[2,8,64,128]{3,2,0,1:T(8,128)}, f32[2,8,64,128]{3,2,0,1:T(8,128)}, u32[]{:S(2)}, u32[]{:S(2)}) %collective-permute-start.4) | collective-permute-done | bytes 524320 | tf_op jit(solution)/shard_map/ppermute | solution.py:12
  245.7 3.1 %collective-permute-start.5 = (f32[1,8,64,128]{3,2,0,1:T(8,128)S(1)}, f32[1,8,64,128]{3,2,0,1:T(8,128)S(1)}, u32[]{:S(2)}, u32[]{:S(2)}) collective-permute-start(f32[1,8,64,128]{3,2,0,1:T(8,128)S(1)} %slice_add_fusion.4), channel_id=1, source_target_pairs={{0,128},{4,132},{8,136},{12,140},{16,144},{20,148},{24,152},{28,15... | collective-permute-start | bytes 786440 | tf_op jit(solution)/shard_map/ppermute | solution.py:12
  248.7 6.3 %multiply_convert_fusion.1 = bf16[8,512,512]{2,1,0:T(8,128)(2,1)S(1)} fusion(f32[8,512]{1,0:T(8,128)} %get-tuple-element.16, f32[8,512]{1,0:T(8,128)} %get-tuple-element.17, f32[8,512]{1,0:T(8,128)} %get-tuple-element.18, f32[8,512]{1,0:T(8,128)S(1)} %get-tuple-element.15, pred[512,512]{1,0:T(8,128)(4,1)} %get-tuple-element.20, ...), kind=kOutput, calls=%fused_computation.3 | convolution fusion | flops 555745280 | bytes 7405568 | tf_op jit(solution)/shard_map/thv,shv->hts/dot_general | solution.py:59
  255.1 2.4 fusion.39
  258.0 1.6 fusion.19
  259.6 2.0 copy.71
  261.7 3.0 %add_convert_fusion = bf16[8,128,512]{2,1,0:T(8,128)(2,1)} fusion(f32[8,128,512]{2,1,0:T(8,128)} %fusion.3, bf16[512,8,64]{0,2,1:T(8,128)(2,1)S(1)} %bitcast.104, bf16[1,8,64,128]{3,2,0,1:T(8,128)(2,1)S(1)} %fusion.39), kind=kOutput, calls=%fused_computation.17 | convolution fusion | flops 68157440 | bytes 3801088 | tf_op jit(solution)/shard_map/fnc,ncd->fnd/dot_general | solution.py:105
  264.7 2.3 copy.72
  267.0 19.8 %fusion.12 = bf16[6,8,64,128]{3,0,2,1:T(8,128)(2,1)S(1)} fusion(f32[64,8,64,128]{3,2,1,0:T(8,128)} %bitcast.100, s32[64]{0:T(128)S(1)} %copy-done.8, s32[6]{0:T(128)S(1)} %copy-done.10, s32[6]{0:T(128)S(1)} %copy-done.9, pred[64]{0:T(512)(128)(4,1)S(1)} %copy-done.11), kind=kOutput, calls=%fused_computation.21 | convolution fusion | flops 302384640 | bytes 17564016 | tf_op jit(solution)/shard_map/nb,nhkv->bhkv/dot_general | solution.py:82
  (62 shorter events, 17.5 us)
Async XLA Ops:
  7.2 2.1 copy-start
  7.2 3.2 %copy-start.6 = (bf16[512,512]{1,0:T(8,128)(2,1)S(1)}, bf16[512,512]{1,0:T(8,128)(2,1)}, u32[]{:S(2)}) copy-start(bf16[512,512]{1,0:T(8,128)(2,1)} %param.8) | copy-start | bytes 1572868
  7.2 3.5 %copy-start.7 = (s32[12,8,512]{2,1,0:T(8,128)S(1)}, s32[12,8,512]{2,1,0:T(8,128)}, u32[]{:S(2)}) copy-start(s32[12,8,512]{2,1,0:T(8,128)} %param.13) | copy-start | bytes 589828
  7.2 4.0 %copy-start.13 = (f32[8,16]{1,0:T(8,128)S(1)}, f32[8,16]{1,0:T(8,128)}, u32[]{:S(2)}) copy-start(f32[8,16]{1,0:T(8,128)} %param.14) | copy-start | bytes 1540
  7.2 45.3 %all-gather.4.cloned.1.call-start = ((), (), s32[]{:S(2)}) async-start(), calls=%async_computation | async-start | bytes 3932160 | tf_op jit(solution)/shard_map/all_gather | solution.py:38
  7.9 259.0 %all-gather.6.cloned.1.call-start = ((), (), s32[]{:S(2)}) async-start(), calls=%async_computation.1 | async-start | bytes 17039360 | tf_op jit(solution)/shard_map/all_gather | solution.py:72
  9.3 4.5 %copy-start.12 = (f32[12]{0:T(128)S(1)}, f32[12]{0:T(128)}, u32[]{:S(2)}) copy-start(f32[12]{0:T(128)} %constant.64.clone) | copy-start | bytes 148
  64.6 3.5 %collective-permute-start = (f32[6,8,64,128]{3,2,0,1:T(8,128)S(1)}, f32[6,8,64,128]{3,2,0,1:T(8,128)S(1)}, u32[]{:S(2)}, u32[]{:S(2)}) collective-permute-start(f32[6,8,64,128]{3,2,0,1:T(8,128)S(1)} %bitcast.106), channel_id=1, source_target_pairs={{0,4},{4,0},{8,12},{12,8},{16,20},{20,16},{24,28},{28,24},{32,36},... | collective-permute-start | bytes 4718600 | tf_op jit(solution)/shard_map/ppermute | solution.py:12
  68.1 42.3 %copy-start.3 = (f32[6,8,64,128]{3,2,0,1:T(8,128)}, f32[6,8,64,128]{3,2,0,1:T(8,128)S(1)}, u32[]{:S(2)}) copy-start(f32[6,8,64,128]{3,2,0,1:T(8,128)S(1)} %collective-permute-done) | copy-start | bytes 4718596
  68.4 40.7 %collective-permute-start.1 = (f32[5,8,64,128]{3,2,0,1:T(8,128)S(1)}, f32[5,8,64,128]{3,2,0,1:T(8,128)S(1)}, u32[]{:S(2)}, u32[]{:S(2)}) collective-permute-start(f32[5,8,64,128]{3,2,0,1:T(8,128)S(1)} %slice_add_fusion), channel_id=1, source_target_pairs={{0,8},{4,12},{8,0},{12,4},{16,24},{20,28},{24,16},{28,20},{32,40},... | collective-permute-start | bytes 3932168 | tf_op jit(solution)/shard_map/ppermute | solution.py:12
  109.1 3.9 %copy-start.4 = (f32[5,8,64,128]{3,2,0,1:T(8,128)}, f32[5,8,64,128]{3,2,0,1:T(8,128)S(1)}, u32[]{:S(2)}) copy-start(f32[5,8,64,128]{3,2,0,1:T(8,128)S(1)} %collective-permute-done.1) | copy-start | bytes 3932164
  110.4 70.4 %collective-permute-start.2 = (f32[4,8,64,128]{3,2,0,1:T(8,128)}, f32[4,8,64,128]{3,2,0,1:T(8,128)}, u32[]{:S(2)}, u32[]{:S(2)}) collective-permute-start(f32[4,8,64,128]{3,2,0,1:T(8,128)} %slice_add_fusion.1), channel_id=1, source_target_pairs={{0,16},{4,20},{8,24},{12,28},{16,0},{20,4},{24,8},{28,12},{32,48},... | collective-permute-start | bytes 3145736 | tf_op jit(solution)/shard_map/ppermute | solution.py:12
  182.3 47.5 %collective-permute-start.3 = (f32[3,8,64,128]{3,2,0,1:T(8,128)S(1)}, f32[3,8,64,128]{3,2,0,1:T(8,128)S(1)}, u32[]{:S(2)}, u32[]{:S(2)}) collective-permute-start(f32[3,8,64,128]{3,2,0,1:T(8,128)S(1)} %slice_add_fusion.2), channel_id=1, source_target_pairs={{0,32},{4,36},{8,40},{12,44},{16,48},{20,52},{24,56},{28,60},{32,0... | collective-permute-start | bytes 2359304 | tf_op jit(solution)/shard_map/ppermute | solution.py:12
  229.8 1.1 copy-start.5
  230.9 13.7 %collective-permute-start.4 = (f32[2,8,64,128]{3,2,0,1:T(8,128)}, f32[2,8,64,128]{3,2,0,1:T(8,128)}, u32[]{:S(2)}, u32[]{:S(2)}) collective-permute-start(f32[2,8,64,128]{3,2,0,1:T(8,128)} %slice_add_fusion.3), channel_id=1, source_target_pairs={{0,64},{4,68},{8,72},{12,76},{16,80},{20,84},{24,88},{28,92},{32,9... | collective-permute-start | bytes 1572872 | tf_op jit(solution)/shard_map/ppermute | solution.py:12
  245.7 9.4 %collective-permute-start.5 = (f32[1,8,64,128]{3,2,0,1:T(8,128)S(1)}, f32[1,8,64,128]{3,2,0,1:T(8,128)S(1)}, u32[]{:S(2)}, u32[]{:S(2)}) collective-permute-start(f32[1,8,64,128]{3,2,0,1:T(8,128)S(1)} %slice_add_fusion.4), channel_id=1, source_target_pairs={{0,128},{4,132},{8,136},{12,140},{16,144},{20,148},{24,152},{28,15... | collective-permute-start | bytes 786440 | tf_op jit(solution)/shard_map/ppermute | solution.py:12
  255.1 4.5 %copy-start.1 = (bf16[8,512,512]{2,1,0:T(8,128)(2,1)}, bf16[8,512,512]{2,1,0:T(8,128)(2,1)S(1)}, u32[]{:S(2)}) copy-start(bf16[8,512,512]{2,1,0:T(8,128)(2,1)S(1)} %multiply_convert_fusion.1) | copy-start | bytes 12582916
  259.6 7.4 %copy-start.8 = (s32[64]{0:T(128)S(1)}, s32[64]{0:T(128)}, u32[]{:S(2)}) copy-start(s32[64]{0:T(128)} %iota_xor_fusion) | copy-start | bytes 772
  259.6 7.4 %copy-start.9 = (s32[6]{0:T(128)S(1)}, s32[6]{0:T(128)}, u32[]{:S(2)}) copy-start(s32[6]{0:T(128)} %get-tuple-element.23) | copy-start | bytes 76
  259.6 7.4 %copy-start.10 = (s32[6]{0:T(128)S(1)}, s32[6]{0:T(128)}, u32[]{:S(2)}) copy-start(s32[6]{0:T(128)} %get-tuple-element.24) | copy-start | bytes 76
  259.6 7.4 %copy-start.11 = (pred[64]{0:T(512)(128)(4,1)S(1)}, pred[64]{0:T(512)(128)(4,1)}, u32[]{:S(2)}) copy-start(pred[64]{0:T(512)(128)(4,1)} %iota_compare_fusion.2) | copy-start | bytes 196
  286.9 2.2 copy-start.2
Sparse Core Ops, SparseCore 0:
  9.9 42.6 all-gather.3
  55.3 164.6 all-gather.5
where the time goes:
time: 299 us; the launch traced here: 298 us
  waiting for transfers between devices  193 us (65%)
  matrix products  55.1 us (18%)
  between operations  14.3 us (5%)
  other arithmetic  14.2 us (5%)
  starting transfers between devices  11.2 us (4%)
  local copies, waits for them, and re-layouts  10.6 us (4%)
    ppermute x6, waiting for transfers between devices, swapped(): lax.ppermute(x, axis, [(i, i ^ 1 << stride) for i in range(lax.axis_size(...  156 us
    all_gather x1, waiting for transfers between devices, per_device(): lax.all_gather(out_grad, 'head', axis=1, tiled=True)  35.9 us
    dot_general x1, matrix products, per_device(): jnp.einsum('nb,nhkv->bhkv', member, piece, precision=lax.Precision.HIGHEST)  19.8 us
    ppermute x6, starting transfers between devices, swapped(): lax.ppermute(x, axis, [(i, i ^ 1 << stride) for i in range(lax.axis_size(...  11.1 us
    unnamed x34, local copies, waits for them, and re-layouts  8.42 us
    dot_general x1, matrix products, per_device(): jnp.einsum('hts,thv->shv', score_mix, dgrad, preferred_element_type=jnp.f...  7.51 us
    dot_general x1, matrix products, per_device(): lax.dot_general(lax.all_gather(out_grad, 'head', axis=1, tiled=True), out...  7.18 us
    dot_general x1, matrix products, per_device(): jnp.einsum('thv,shv->hts', dgrad, value_product, preferred_element_type=j...  6.34 us
  transfers between devices with their start and end apart: 8, of which 6 were waited for; matrix products, arithmetic and copies ran while one was open for 19% of the time, Pallas kernels for 0%

commit v1 on v0

v1 whole, which is shorter than its diff:
```python
import jax
import jax.numpy as jnp
from jax import lax
from jax.experimental import pallas as pl
from jax.experimental.pallas import tpu as pltpu
from jax.sharding import PartitionSpec as P

DK = 64
DV = 128
BLK = 64
LB = 3
SEQ_BITS = 6
ROWS = 512
HEADS = 8
PAIRS = 4
FEAT = 768
CHUNKS = 4
CROWS = ROWS // CHUNKS
HALF = 256
SLICE = 32
SCALES = [float((DK * BLK * 2 ** max(level - 1, 0)) ** -0.5) for level in range(LB + 1 + SEQ_BITS)]

F32 = jnp.float32
BF16 = jnp.bfloat16

S0, S1, S2, S4, R0, R1, R2, R3, R4, N_SEM = 0, 1, 8, 11, 12, 14, 21, 24, 31, 32


def nt(a, b):
    return lax.dot_general(a, b, (((1,), (1,)), ((), ())), preferred_element_type=F32)


def nn(a, b):
    return lax.dot_general(a, b, (((1,), (0,)), ((), ())), preferred_element_type=F32)


def flipped(value, mask, bits):
    out = value
    for k in range(bits):
        if mask >> k & 1:
            out = out + (1 - 2 * ((value // 2**k) % 2)) * 2**k
    return out


def kernel(
    q_hbm, k_hbm, v_hbm, og_hbm, w_hbm, codes_ref, table_ref,
    qo_hbm, ko_hbm, vo_hbm,
    qp, kp, vp, w4, gath, dout, kT, qT, lam, inner, sm,
    gsb, pgs, zbuf, xbuf, state_low,
    lg, rb0, rbh, rsrc, rbuf, tsrc, tbuf, rets, rfin,
    kacc, vacc, qo, ko, vo,
    loc_sem, out_sem, ys, yr, ss, sr,
):
    g = lax.axis_index("seq")
    y = lax.axis_index("head")
    c = g % 2
    z = (g // 2) % 8
    x = g // 16
    right, left, across = (y + 1) % 4, (y + 3) % 4, (y + 2) % 4

    def z_peer(i):
        return (x * 16 + flipped(z, i, 3) * 2 + c, y)

    def x_peer(i):
        return (flipped(x, i, 2) * 16 + z * 2 + c, y)

    partner = (g + 1 - 2 * c, y)
    peers = [partner, (g, right), (g, left)]
    peers += [z_peer(i) for i in range(1, 8)] + [x_peer(i) for i in range(1, 4)]

    loads = []
    for p in range(PAIRS):
        loads.append(pltpu.make_async_copy(k_hbm.at[:, pl.ds(p * 128, 128)], kp.at[p], loc_sem.at[len(loads)]))
    for p in range(PAIRS):
        loads.append(pltpu.make_async_copy(v_hbm.at[:, pl.ds(p * 256, 256)], vp.at[p], loc_sem.at[len(loads)]))
    for p in range(PAIRS):
        loads.append(pltpu.make_async_copy(q_hbm.at[:, pl.ds(p * 128, 128)], qp.at[p], loc_sem.at[len(loads)]))
    loads.append(pltpu.make_async_copy(og_hbm, gath.at[y], loc_sem.at[len(loads)]))
    for p in range(4):
        loads.append(pltpu.make_async_copy(w_hbm.at[:, pl.ds(p * FEAT, FEAT)], w4.at[p], loc_sem.at[len(loads)]))
    for load in loads:
        load.start()

    barrier = pltpu.get_barrier_semaphore()
    for peer in peers:
        pl.semaphore_signal(barrier, inc=1, device_id=peer, device_id_type=pl.DeviceIdType.MESH)
    pl.semaphore_wait(barrier, len(peers))

    def remote(src, dst, send, recv, slot, to):
        return pltpu.make_async_remote_copy(
            src_ref=src, dst_ref=dst, send_sem=send.at[slot], recv_sem=recv.at[slot],
            device_id=to, device_id_type=pl.DeviceIdType.MESH,
        )

    def own(j):
        rows = pl.ds(j * CROWS, CROWS)
        return [
            remote(og_hbm.at[rows], gath.at[y, rows], ys, yr, j, (g, right)),
            remote(og_hbm.at[rows], gath.at[y, rows], ys, yr, 4 + j, (g, left)),
        ]

    def forward(j):
        first = pl.ds(j * CROWS, CROWS // 2)
        second = pl.ds(j * CROWS + CROWS // 2, CROWS // 2)
        return [
            remote(gath.at[left, first], gath.at[left, first], ys, yr, 8 + j, (g, right)),
            remote(gath.at[right, second], gath.at[right, second], ys, yr, 12 + j, (g, left)),
        ]

    def start(copies):
        for copy in copies:
            copy.start()
        sent.extend(copies)
        return copies

    def arrive(copies):
        for copy in copies:
            copy.wait_recv()

    sent = []
    owns = [own(j) for j in range(CHUNKS)]
    forwards = [forward(j) for j in range(CHUNKS)]
    start(owns[0])
    start(owns[1])

    for load in loads[:8]:
        load.wait()

    def states_of(p, _):
        kT[p] = kp[p].T
        both = nn(kT[p], vp[p])
        at = pl.multiple_of(p * 128, 128)
        gsb[pl.ds(at, 64), :] = both[:64, :128]
        gsb[pl.ds(at + 64, 64), :] = both[64:, 128:]
        return 0

    lax.fori_loop(0, PAIRS, states_of, 0)
    s0 = start([remote(gsb, pgs, ss, sr, S0, partner)])

    table = table_ref[...]
    columns = [jnp.broadcast_to(table[:, j:j + 1], (HEADS, ROWS)) for j in range(16)]
    for level in range(LB + 1 + SEQ_BITS):
        codes = codes_ref[level]
        looked = jnp.zeros((HEADS, ROWS), F32)
        for j in range(16):
            looked = jnp.where(codes == j, columns[j], looked)
        looked = looked * SCALES[level]
        if level > LB:
            looked = looked * ((g // 2 ** (level - LB - 1)) % 2).astype(F32)
        lam[level] = looked
    token_block = lax.broadcasted_iota(jnp.int32, (HEADS, ROWS), 1) // BLK
    for cs in range(ROWS // BLK):
        line = jnp.zeros((HEADS, ROWS), F32)
        for ct in range(cs, ROWS // BLK):
            line = jnp.where(token_block == ct, lam[(ct ^ cs).bit_length()], line)
        inner[cs] = line

    for load in loads[8:12]:
        load.wait()

    def turned(p, _):
        qT[p] = qp[p].T
        return 0

    lax.fori_loop(0, PAIRS, turned, 0)

    mine = pl.ds(pl.multiple_of(c * HALF, HALF), HALF)
    other = pl.ds(pl.multiple_of((1 - c) * HALF, HALF), HALF)
    arrive(s0)
    zbuf[0] = (gsb[mine, :] + pgs[mine, :]).astype(BF16)
    s1 = start([remote(zbuf.at[0], zbuf.at[i], ss, sr, S1 + i - 1, z_peer(i)) for i in range(1, 8)])
    state_low[0] = pgs[...].astype(BF16)

    def turn(j):
        arrive(owns[j])
        start(forwards[j])
        if j + 2 < CHUNKS:
            start(owns[j + 2])

    def mix_of(h, s0_, count, t0_, width):
        lines = [
            jnp.broadcast_to(inner[s0_ // BLK + i, pl.ds(h, 1), pl.ds(t0_, width)], (BLK, width))
            for i in range(count // BLK)
        ]
        mix = jnp.concatenate(lines, axis=0)
        s_at = lax.broadcasted_iota(jnp.int32, (count, width), 0) + s0_
        t_at = lax.broadcasted_iota(jnp.int32, (count, width), 1) + t0_
        return jnp.where(s_at <= t_at, mix, 0.0)

    def masked(pair, e):
        lane = lax.broadcasted_iota(jnp.int32, pair.shape, 1)
        return jnp.where((lane >= 64) == (e == 1), pair, jnp.zeros_like(pair))

    def scores_of(p, _):
        for e in range(2):
            h = 2 * p + e
            keys = masked(kp[p], e)
            query = qp[p]
            sm[h, pl.ds(0, HALF), :] = (mix_of(h, 0, HALF, 0, ROWS) * nt(keys[:HALF], query)).astype(BF16)
            sm[h, pl.ds(HALF, HALF), pl.ds(HALF, HALF)] = (
                mix_of(h, HALF, HALF, HALF, HALF) * nt(keys[HALF:], query[HALF:])
            ).astype(BF16)
        return 0

    turn(0)
    lax.fori_loop(0, 2, scores_of, 0)
    turn(1)
    lax.fori_loop(2, 4, scores_of, 0)

    arrive(s1)
    parts = [zbuf[i].astype(F32) for i in range(8)]
    pair1 = parts[2] + parts[3]
    quad = (parts[4] + parts[5]) + (parts[6] + parts[7])
    xbuf[0] = ((parts[0] + parts[1]) + pair1 + quad).astype(BF16)
    s2 = start([remote(xbuf.at[0], xbuf.at[i], ss, sr, S2 + i - 1, x_peer(i)) for i in range(1, 4)])
    state_low[1, mine, :] = zbuf[1]
    state_low[2, mine, :] = pair1.astype(BF16)
    state_low[3, mine, :] = quad.astype(BF16)

    turn(2)
    arrive(s2)
    state_low[4, mine, :] = xbuf[1]
    state_low[5, mine, :] = (xbuf[2].astype(F32) + xbuf[3].astype(F32)).astype(BF16)
    s4 = start([remote(state_low.at[pl.ds(1, 5), mine], state_low.at[pl.ds(1, 5), mine], ss, sr, S4, partner)])

    for load in loads[12:]:
        load.wait()
    arrive(forwards[0])
    arrive(forwards[1])

    def project(first):
        def tile(n, _):
            cols = pl.ds(pl.multiple_of(n * 256, 256), 256)
            total = None
            for d in range(4):
                part = nt(gath[d, pl.ds(first, HALF), :], w4[d, cols, :])
                total = part if total is None else total + part
            low = total.astype(BF16)
            dout[2 * n, pl.ds(first, HALF), :] = low[:, :128]
            dout[2 * n + 1, pl.ds(first, HALF), :] = low[:, 128:]
            return 0

        lax.fori_loop(0, 4, tile, 0)

    project(0)
    turn(3)
    arrive(forwards[2])
    arrive(forwards[3])
    project(HALF)

    def level_grads(p, _):
        turned_q = qT[p].astype(F32)
        for e in range(2):
            h = 2 * p + e
            rows = turned_q[e * 64:(e + 1) * 64, :]
            scaled = [
                (lam[LB + 1 + b, pl.ds(h, 1), :] * rows).astype(BF16) for b in range(SEQ_BITS)
            ]
            grads = nn(jnp.concatenate(scaled, axis=0), dout[h]).astype(BF16)
            at = pl.ds(pl.multiple_of(h * 64, 64), 64)
            for b in range(SEQ_BITS):
                lg[b, at, :] = grads[b * 64:(b + 1) * 64, :]
        return 0

    lax.fori_loop(0, PAIRS, level_grads, 0)
    r0 = start([
        remote(lg.at[pl.ds(1, 5), other], rbh, ss, sr, R0, partner),
        remote(lg.at[0], rb0, ss, sr, R0 + 1, partner),
    ])
    arrive(s4)

    def attention(p, _):
        turned_k = kT[p]
        values = vp[p]
        query = qp[p]
        lines = []
        for e in range(2):
            h = 2 * p + e
            mine_q = masked(query, e)
            d = dout[h]
            mine_v = values[:, e * 128:(e + 1) * 128]
            low = (mix_of(h, 0, HALF, 0, ROWS) * nt(mine_v[:HALF], d)).astype(BF16)
            high = (mix_of(h, HALF, HALF, HALF, HALF) * nt(mine_v[HALF:], d[HALF:])).astype(BF16)
            key_low = nn(low, mine_q)
            key_high = nn(high, mine_q[HALF:])
            if e == 0:
                kacc[p, pl.ds(0, HALF), :] = key_low
                kacc[p, pl.ds(HALF, HALF), :] = key_high
            else:
                kacc[p, pl.ds(0, HALF), :] += key_low
                kacc[p, pl.ds(HALF, HALF), :] += key_high
            vacc[p, pl.ds(0, HALF), pl.ds(e * 128, 128)] = nn(sm[h, pl.ds(0, HALF), :], d)
            vacc[p, pl.ds(HALF, HALF), pl.ds(e * 128, 128)] = nn(
                sm[h, pl.ds(HALF, HALF), pl.ds(HALF, HALF)], d[HALF:]
            )
            own_k = turned_k[e * 64:(e + 1) * 64, :]
            line = nn(own_k[:, :HALF], low)
            line_high = nn(own_k[:, HALF:], high)
            at = pl.ds(pl.multiple_of(h * 64, 64), 64)
            states = state_low[:, at, :].reshape(SEQ_BITS * 64, 128)
            read = nt(states, d)
            for b in range(SEQ_BITS):
                line = line + lam[LB + 1 + b, pl.ds(h, 1), :] * read[b * 64:(b + 1) * 64, :]
            lines.append(jnp.concatenate([line[:, :HALF], line[:, HALF:] + line_high], axis=1))
        qo[p] = jnp.concatenate(lines, axis=0).T.astype(BF16)
        return 0

    lax.fori_loop(0, 1, attention, 0)
    arrive(r0)
    rsrc[...] = (lg[pl.ds(1, 5), mine, :].astype(F32) + rbh[...].astype(F32)).astype(BF16)

    def owned(at):
        return pl.ds(pl.multiple_of(at * SLICE, SLICE), SLICE)

    r1 = start([
        remote(rsrc.at[:, owned(flipped(z, i, 3))], rbuf.at[i], ss, sr, R1 + i - 1, z_peer(i))
        for i in range(1, 8)
    ])
    rbuf[0] = rsrc[:, owned(z), :]

    lax.fori_loop(1, 3, attention, 0)
    arrive(r1)
    tops = rbuf[0, pl.ds(3, 2)].astype(F32)
    for i in range(1, 8):
        tops = tops + rbuf[i, pl.ds(3, 2)].astype(F32)
    tsrc[...] = tops.astype(BF16)
    r2 = start([remote(tsrc, tbuf.at[i], ss, sr, R2 + i - 1, x_peer(i)) for i in range(1, 4)])

    lax.fori_loop(3, 4, attention, 0)
    arrive(r2)
    outer = tbuf[1, 0].astype(F32) + tbuf[2, 1].astype(F32) + tbuf[3, 1].astype(F32)
    for r in range(8):
        total = outer
        for i in range(1, 8):
            total = total + rbuf[r ^ i, i.bit_length() - 1].astype(F32)
        rets[r] = total.astype(BF16)
    finals = pl.ds(pl.multiple_of(c * HALF + z * SLICE, SLICE), SLICE)
    r3 = start([remote(rets.at[i], rfin.at[finals], ss, sr, R3 + i - 1, z_peer(i)) for i in range(1, 8)])
    rfin[finals, :] = rets[0]

    outs = []
    for p in range(PAIRS):
        outs.append(pltpu.make_async_copy(qo.at[p], qo_hbm.at[:, pl.ds(p * 128, 128)], out_sem.at[p]))
        outs[-1].start()

    arrive(r3)
    r4 = start([remote(rfin.at[mine], rfin.at[mine], ss, sr, R4, partner)])
    arrive(r4)

    for p in range(PAIRS):
        back = (rfin[pl.ds(p * 128, 128), :].astype(F32) + rb0[pl.ds(p * 128, 128), :].astype(F32)).astype(BF16)
        zero = jnp.zeros((64, 128), BF16)
        spread = jnp.concatenate([
            jnp.concatenate([back[:64], zero], axis=1),
            jnp.concatenate([zero, back[64:]], axis=1),
        ], axis=0)
        ko[p] = (kacc[p] + nt(vp[p], spread)).astype(BF16)
        outs.append(pltpu.make_async_copy(ko.at[p], ko_hbm.at[:, pl.ds(p * 128, 128)], out_sem.at[4 + p]))
        outs[-1].start()
        vo[p] = (vacc[p] + nn(kp[p], spread)).astype(BF16)
        outs.append(pltpu.make_async_copy(vo.at[p], vo_hbm.at[:, pl.ds(p * 256, 256)], out_sem.at[8 + p]))
        outs[-1].start()

    for copy in sent:
        copy.wait_send()
    for copy in outs:
        copy.wait()


def per_device(query_rows, key_rows, value_rows, out_grad, out_weight, level_codes, level_table):
    any_space = pl.BlockSpec(memory_space=pl.ANY)
    vmem = pl.BlockSpec(memory_space=pltpu.VMEM)
    scratch = [
        pltpu.VMEM((PAIRS, ROWS, 128), BF16),
        pltpu.VMEM((PAIRS, ROWS, 128), BF16),
        pltpu.VMEM((PAIRS, ROWS, 256), BF16),
        pltpu.VMEM((4, HEADS * DV, FEAT), BF16),
        pltpu.VMEM((4, ROWS, FEAT), BF16),
        pltpu.VMEM((HEADS, ROWS, DV), BF16),
        pltpu.VMEM((PAIRS, 128, ROWS), BF16),
        pltpu.VMEM((PAIRS, 128, ROWS), BF16),
        pltpu.VMEM((LB + 1 + SEQ_BITS, HEADS, ROWS), F32),
        pltpu.VMEM((ROWS // BLK, HEADS, ROWS), F32),
        pltpu.VMEM((HEADS, ROWS, ROWS), BF16),
        pltpu.VMEM((ROWS, 128), F32),
        pltpu.VMEM((ROWS, 128), F32),
        pltpu.VMEM((8, HALF, 128), BF16),
        pltpu.VMEM((4, HALF, 128), BF16),
        pltpu.VMEM((SEQ_BITS, ROWS, 128), BF16),
        pltpu.VMEM((SEQ_BITS, ROWS, 128), BF16),
        pltpu.VMEM((ROWS, 128), BF16),
        pltpu.VMEM((5, HALF, 128), BF16),
        pltpu.VMEM((5, HALF, 128), BF16),
        pltpu.VMEM((8, 5, SLICE, 128), BF16),
        pltpu.VMEM((2, SLICE, 128), BF16),
        pltpu.VMEM((4, 2, SLICE, 128), BF16),
        pltpu.VMEM((8, SLICE, 128), BF16),
        pltpu.VMEM((ROWS, 128), BF16),
        pltpu.VMEM((PAIRS, ROWS, 128), F32),
        pltpu.VMEM((PAIRS, ROWS, 256), F32),
        pltpu.VMEM((PAIRS, ROWS, 128), BF16),
        pltpu.VMEM((PAIRS, ROWS, 128), BF16),
        pltpu.VMEM((PAIRS, ROWS, 256), BF16),
        pltpu.SemaphoreType.DMA((17,)),
        pltpu.SemaphoreType.DMA((12,)),
        pltpu.SemaphoreType.DMA((16,)),
        pltpu.SemaphoreType.DMA((16,)),
        pltpu.SemaphoreType.DMA((N_SEM,)),
        pltpu.SemaphoreType.DMA((N_SEM,)),
    ]
    return pl.pallas_call(
        kernel,
        out_shape=(
            jax.ShapeDtypeStruct((ROWS, HEADS * DK), BF16),
            jax.ShapeDtypeStruct((ROWS, HEADS * DK), BF16),
            jax.ShapeDtypeStruct((ROWS, HEADS * DV), BF16),
        ),
        in_specs=[any_space] * 5 + [vmem] * 2,
        out_specs=(any_space,) * 3,
        scratch_shapes=scratch,
        compiler_params=pltpu.CompilerParams(
            collective_id=0, has_side_effects=True, vmem_limit_bytes=56 * 1024 * 1024
        ),
        cost_estimate=pl.CostEstimate(flops=8_000_000_000, bytes_accessed=12_000_000, transcendentals=0),
    )(query_rows, key_rows, value_rows, out_grad, out_weight, level_codes, level_table)


def solution(mesh):
    return jax.shard_map(
        per_device,
        mesh=mesh,
        in_specs=(
            P("seq", "head"),
            P("seq", "head"),
            P("seq", "head"),
            P("seq", "head"),
            P("head", None),
            P(None, "head", "seq"),
            P("head", None),
        ),
        out_specs=(P("seq", "head"), P("seq", "head"), P("seq", "head")),
        check_vma=False,
    )
```

time: 299 us -> 76.4 us (0.26)
  the two profiles are of different devices: /device:TPU:56 before, /device:TPU:1 now
where the time goes in v1:
time: 76.4 us; the launch traced here: 76.1 us
  Pallas kernels  69.5 us (91%)
  local copies, waits for them, and re-layouts  6 us (8%)
    pallas_call x1, Pallas kernels, per_device(): pl.pallas_call(kernel, out_shape=(jax.ShapeDtypeStruct((ROWS, HEADS * DK)...  69.5 us
    unnamed x3, local copies, waits for them, and re-layouts  6 us

profile of v1, /device:TPU:1, one launch (start us, length us, event | category | flops | bytes accessed | tf_op | source)
XLA Modules:
  0.0 76.1 jit_solution(8366381625668986223)
XLA Ops:
  0.6 69.5 %shard_map.94 = (bf16[512,512]{1,0:T(8,128)(2,1)}, bf16[512,512]{1,0:T(8,128)(2,1)}, bf16[512,1024]{1,0:T(8,128)(2,1)}) custom-call(bf16[512,512]{1,0:T(8,128)(2,1)} %q_hbm.1, bf16[512,512]{1,0:T(8,128)(2,1)} %k_hbm.1, bf16[512,1024]{1,0:T(8,128)(2,1)} %v_hbm.1, bf16[512,768]{1,0:T(8,128)(2,1)} %og_hbm.1, bf16[1024,3072]{1,0:T(8,128)(2,1)} %w_hbm.1, ...), custom_call_target="tpu_custom_call" | custom-call | flops 8000000000 | bytes 12000000 | tf_op jit(solution)/shard_map/pallas_call | solution.py:411
  70.1 1.9 %copy.13 = bf16[512,512]{1,0:T(8,128)(2,1)} copy(bf16[512,512]{1,0:T(8,128)(2,1)} %get-tuple-element.6) | data formatting | bytes 1048576
  72.0 1.9 %copy.14 = bf16[512,512]{1,0:T(8,128)(2,1)} copy(bf16[512,512]{1,0:T(8,128)(2,1)} %get-tuple-element.7) | data formatting | bytes 1048576
  73.9 2.3 %copy.15 = bf16[512,1024]{1,0:T(8,128)(2,1)} copy(bf16[512,1024]{1,0:T(8,128)(2,1)} %get-tuple-element.8) | data formatting | bytes 2097152

commit v2 on v1

--- a/solution.py
+++ b/solution.py
@@ -23,7 +23,7 @@
 F32 = jnp.float32
 BF16 = jnp.bfloat16
 
-S0, S1, S2, S4, R0, R1, R2, R3, R4, N_SEM = 0, 1, 8, 11, 12, 14, 21, 24, 31, 32
+S0, S1, S2, S4, R0, R1, R2, R3, R4, N_SEM = 0, 1, 8, 11, 16, 27, 41, 44, 51, 52
 
 
 def nt(a, b):
@@ -44,11 +44,11 @@
 
 def kernel(
     q_hbm, k_hbm, v_hbm, og_hbm, w_hbm, codes_ref, table_ref,
-    qo_hbm, ko_hbm, vo_hbm,
+    qo_hbm, ko_hbm, vo_hbm, ret_ref,
     qp, kp, vp, w4, gath, dout, kT, qT, lam, inner, sm,
     gsb, pgs, zbuf, xbuf, state_low,
     lg, rb0, rbh, rsrc, rbuf, tsrc, tbuf, rets, rfin,
-    kacc, vacc, qo, ko, vo,
+    kacc, vacc, qo, pacc, lgacc,
     loc_sem, out_sem, ys, yr, ss, sr,
 ):
     g = lax.axis_index("seq")
@@ -84,6 +84,19 @@
     barrier = pltpu.get_barrier_semaphore()
     for peer in peers:
         pl.semaphore_signal(barrier, inc=1, device_id=peer, device_id_type=pl.DeviceIdType.MESH)
+
+    for load in loads[:8]:
+        load.wait()
+
+    def states_of(p, _):
+        kT[p] = kp[p].T
+        both = nn(kT[p], vp[p])
+        at = pl.multiple_of(p * 128, 128)
+        gsb[pl.ds(at, 64), :] = both[:64, :128]
+        gsb[pl.ds(at + 64, 64), :] = both[64:, 128:]
+        return 0
+
+    lax.fori_loop(0, PAIRS, states_of, 0)
     pl.semaphore_wait(barrier, len(peers))
 
     def remote(src, dst, send, recv, slot, to):
@@ -120,21 +133,8 @@
     sent = []
     owns = [own(j) for j in range(CHUNKS)]
     forwards = [forward(j) for j in range(CHUNKS)]
-    start(owns[0])
-    start(owns[1])
-
-    for load in loads[:8]:
-        load.wait()
-
-    def states_of(p, _):
-        kT[p] = kp[p].T
-        both = nn(kT[p], vp[p])
-        at = pl.multiple_of(p * 128, 128)
-        gsb[pl.ds(at, 64), :] = both[:64, :128]
-        gsb[pl.ds(at + 64, 64), :] = both[64:, 128:]
-        return 0
-
-    lax.fori_loop(0, PAIRS, states_of, 0)
+    for j in range(CHUNKS):
+        start(owns[j])
     s0 = start([remote(gsb, pgs, ss, sr, S0, partner)])
 
     table = table_ref[...]
@@ -174,8 +174,6 @@
     def turn(j):
         arrive(owns[j])
         start(forwards[j])
-        if j + 2 < CHUNKS:
-            start(owns[j + 2])
 
     def mix_of(h, s0_, count, t0_, width):
         lines = [
@@ -202,10 +200,55 @@
             ).astype(BF16)
         return 0
 
+    lax.fori_loop(0, PAIRS, scores_of, 0)
+
+    def project(slots, first, count, begin, end):
+        def tile(n, _):
+            cols = pl.ds(pl.multiple_of(n * 256, 256), 256)
+            rows = pl.ds(first, count)
+            total = None if begin else pacc[n, rows, :]
+            for d in slots:
+                part = nt(gath[d, rows, :], w4[d, cols, :])
+                total = part if total is None else total + part
+            if end:
+                low = total.astype(BF16)
+                dout[2 * n, rows, :] = low[:, :128]
+                dout[2 * n + 1, rows, :] = low[:, 128:]
+            else:
+                pacc[n, rows, :] = total
+            return 0
+
+        lax.fori_loop(0, 4, tile, 0)
+
+    def level_part(p, e, first):
+        h = 2 * p + e
+        rows = qT[p, e * 64:(e + 1) * 64, first:first + HALF].astype(F32)
+        scaled = [
+            (lam[LB + 1 + b, pl.ds(h, 1), first:first + HALF] * rows).astype(BF16) for b in range(SEQ_BITS)
+        ]
+        return nn(jnp.concatenate(scaled, axis=0), dout[h, first:first + HALF, :])
+
+    def level_first(p, _):
+        for e in range(2):
+            lgacc[p, e] = level_part(p, e, 0)
+        return 0
+
+    def level_rest(p, _):
+        for e in range(2):
+            grads = (lgacc[p, e] + level_part(p, e, HALF)).astype(BF16)
+            at = pl.ds(pl.multiple_of(p * 128 + e * 64, 64), 64)
+            for b in range(SEQ_BITS):
+                lg[b, at, :] = grads[b * 64:(b + 1) * 64, :]
+        return 0
+
+    for load in loads[12:]:
+        load.wait()
+    project([y], 0, ROWS, True, False)
     turn(0)
-    lax.fori_loop(0, 2, scores_of, 0)
     turn(1)
-    lax.fori_loop(2, 4, scores_of, 0)
+    project([left, right], 0, HALF, False, False)
+    turn(2)
+    turn(3)
 
     arrive(s1)
     parts = [zbuf[i].astype(F32) for i in range(8)]
@@ -217,56 +260,50 @@
     state_low[2, mine, :] = pair1.astype(BF16)
     state_low[3, mine, :] = quad.astype(BF16)
 
-    turn(2)
+    project([left, right], HALF, HALF, False, False)
+    arrive(forwards[0])
+    arrive(forwards[1])
+    project([across], 0, HALF, False, True)
+    lax.fori_loop(0, PAIRS, level_first, 0)
+
     arrive(s2)
     state_low[4, mine, :] = xbuf[1]
     state_low[5, mine, :] = (xbuf[2].astype(F32) + xbuf[3].astype(F32)).astype(BF16)
-    s4 = start([remote(state_low.at[pl.ds(1, 5), mine], state_low.at[pl.ds(1, 5), mine], ss, sr, S4, partner)])
-
-    for load in loads[12:]:
-        load.wait()
-    arrive(forwards[0])
-    arrive(forwards[1])
-
-    def project(first):
-        def tile(n, _):
-            cols = pl.ds(pl.multiple_of(n * 256, 256), 256)
-            total = None
-            for d in range(4):
-                part = nt(gath[d, pl.ds(first, HALF), :], w4[d, cols, :])
-                total = part if total is None else total + part
-            low = total.astype(BF16)
-            dout[2 * n, pl.ds(first, HALF), :] = low[:, :128]
-            dout[2 * n + 1, pl.ds(first, HALF), :] = low[:, 128:]
-            return 0
-
-        lax.fori_loop(0, 4, tile, 0)
-
-    project(0)
-    turn(3)
+    s4 = start([
+        remote(state_low.at[b, mine], state_low.at[b, mine], ss, sr, S4 + b - 1, partner) for b in range(1, SEQ_BITS)
+    ])
+
     arrive(forwards[2])
     arrive(forwards[3])
-    project(HALF)
-
-    def level_grads(p, _):
-        turned_q = qT[p].astype(F32)
-        for e in range(2):
-            h = 2 * p + e
-            rows = turned_q[e * 64:(e + 1) * 64, :]
-            scaled = [
-                (lam[LB + 1 + b, pl.ds(h, 1), :] * rows).astype(BF16) for b in range(SEQ_BITS)
-            ]
-            grads = nn(jnp.concatenate(scaled, axis=0), dout[h]).astype(BF16)
-            at = pl.ds(pl.multiple_of(h * 64, 64), 64)
-            for b in range(SEQ_BITS):
-                lg[b, at, :] = grads[b * 64:(b + 1) * 64, :]
-        return 0
-
-    lax.fori_loop(0, PAIRS, level_grads, 0)
-    r0 = start([
-        remote(lg.at[pl.ds(1, 5), other], rbh, ss, sr, R0, partner),
-        remote(lg.at[0], rb0, ss, sr, R0 + 1, partner),
+    project([across], HALF, HALF, False, True)
+
+    r0 = []
+    for i in range(2):
+        p = 2 * (1 - c) + i
+        level_rest(p, 0)
+        rows = pl.ds(pl.multiple_of(p * 128, 128), 128)
+        r0 += start([
+            remote(lg.at[1 + b, rows], rbh.at[b, pl.ds(i * 128, 128)], ss, sr, R0 + 5 * i + b, partner)
+            for b in range(5)
+        ])
+    for i in range(2):
+        level_rest(2 * c + i, 0)
+    arrive(r0)
+    rsrc[...] = (lg[pl.ds(1, 5), mine, :].astype(F32) + rbh[...].astype(F32)).astype(BF16)
+
+    def owned(at):
+        return pl.ds(pl.multiple_of(at * SLICE, SLICE), SLICE)
+
+    r1x = start([
+        remote(rsrc.at[pl.ds(3, 2), owned(flipped(z, i, 3))], rbuf.at[i, pl.ds(3, 2)], ss, sr, R1 + i - 1, z_peer(i))
+        for i in range(1, 8)
     ])
+    r1 = start([
+        remote(rsrc.at[pl.ds(0, 3), owned(flipped(z, i, 3))], rbuf.at[i, pl.ds(0, 3)], ss, sr, R1 + 6 + i, z_peer(i))
+        for i in range(1, 8)
+    ])
+    rbuf[0] = rsrc[:, owned(z), :]
+    rb = start([remote(lg.at[0], rb0, ss, sr, R0 + 10, partner)])
     arrive(s4)
 
     def attention(p, _):
@@ -305,28 +342,32 @@
         qo[p] = jnp.concatenate(lines, axis=0).T.astype(BF16)
         return 0
 
-    lax.fori_loop(0, 1, attention, 0)
-    arrive(r0)
-    rsrc[...] = (lg[pl.ds(1, 5), mine, :].astype(F32) + rbh[...].astype(F32)).astype(BF16)
-
-    def owned(at):
-        return pl.ds(pl.multiple_of(at * SLICE, SLICE), SLICE)
-
-    r1 = start([
-        remote(rsrc.at[:, owned(flipped(z, i, 3))], rbuf.at[i], ss, sr, R1 + i - 1, z_peer(i))
-        for i in range(1, 8)
-    ])
-    rbuf[0] = rsrc[:, owned(z), :]
-
-    lax.fori_loop(1, 3, attention, 0)
-    arrive(r1)
+    def store(p):
+        copies = [
+            pltpu.make_async_copy(qo.at[p], qo_hbm.at[p], out_sem.at[p]),
+            pltpu.make_async_copy(kacc.at[p], ko_hbm.at[p], out_sem.at[4 + p]),
+            pltpu.make_async_copy(vacc.at[p], vo_hbm.at[p], out_sem.at[8 + p]),
+        ]
+        for copy in copies:
+            copy.start()
+        outs.extend(copies)
+
+    outs = []
+
+    lax.fori_loop(0, 2, attention, 0)
+    store(0)
+    store(1)
+    arrive(r1x)
     tops = rbuf[0, pl.ds(3, 2)].astype(F32)
     for i in range(1, 8):
         tops = tops + rbuf[i, pl.ds(3, 2)].astype(F32)
     tsrc[...] = tops.astype(BF16)
     r2 = start([remote(tsrc, tbuf.at[i], ss, sr, R2 + i - 1, x_peer(i)) for i in range(1, 4)])
 
-    lax.fori_loop(3, 4, attention, 0)
+    lax.fori_loop(2, 4, attention, 0)
+    store(2)
+    store(3)
+    arrive(r1)
     arrive(r2)
     outer = tbuf[1, 0].astype(F32) + tbuf[2, 1].astype(F32) + tbuf[3, 1].astype(F32)
     for r in range(8):
@@ -337,34 +378,27 @@
     finals = pl.ds(pl.multiple_of(c * HALF + z * SLICE, SLICE), SLICE)
     r3 = start([remote(rets.at[i], rfin.at[finals], ss, sr, R3 + i - 1, z_peer(i)) for i in range(1, 8)])
     rfin[finals, :] = rets[0]
-
-    outs = []
-    for p in range(PAIRS):
-        outs.append(pltpu.make_async_copy(qo.at[p], qo_hbm.at[:, pl.ds(p * 128, 128)], out_sem.at[p]))
-        outs[-1].start()
-
+    arrive(rb)
     arrive(r3)
     r4 = start([remote(rfin.at[mine], rfin.at[mine], ss, sr, R4, partner)])
+    for copy in outs:
+        copy.wait()
     arrive(r4)
-
-    for p in range(PAIRS):
-        back = (rfin[pl.ds(p * 128, 128), :].astype(F32) + rb0[pl.ds(p * 128, 128), :].astype(F32)).astype(BF16)
-        zero = jnp.zeros((64, 128), BF16)
-        spread = jnp.concatenate([
-            jnp.concatenate([back[:64], zero], axis=1),
-            jnp.concatenate([zero, back[64:]], axis=1),
-        ], axis=0)
-        ko[p] = (kacc[p] + nt(vp[p], spread)).astype(BF16)
-        outs.append(pltpu.make_async_copy(ko.at[p], ko_hbm.at[:, pl.ds(p * 128, 128)], out_sem.at[4 + p]))
-        outs[-1].start()
-        vo[p] = (vacc[p] + nn(kp[p], spread)).astype(BF16)
-        outs.append(pltpu.make_async_copy(vo.at[p], vo_hbm.at[:, pl.ds(p * 256, 256)], out_sem.at[8 + p]))
-        outs[-1].start()
-
+    ret_ref[...] = (rfin[...].astype(F32) + rb0[...].astype(F32)).astype(BF16)
     for copy in sent:
         copy.wait_send()
-    for copy in outs:
-        copy.wait()
+
+
+def finish(ret_ref, k_ref, v_ref, q_ref, kacc_ref, vacc_ref, qo_ref, ko_ref, vo_ref):
+    back = ret_ref[...]
+    zero = jnp.zeros((64, 128), BF16)
+    spread = jnp.concatenate([
+        jnp.concatenate([back[:64], zero], axis=1),
+        jnp.concatenate([zero, back[64:]], axis=1),
+    ], axis=0)
+    qo_ref[...] = q_ref[0]
+    ko_ref[...] = (kacc_ref[0] + nt(v_ref[...], spread)).astype(BF16)
+    vo_ref[...] = (vacc_ref[0] + nn(k_ref[...], spread)).astype(BF16)
 
 
 def per_device(query_rows, key_rows, value_rows, out_grad, out_weight, level_codes, level_table):
@@ -399,8 +433,8 @@
         pltpu.VMEM((PAIRS, ROWS, 128), F32),
         pltpu.VMEM((PAIRS, ROWS, 256), F32),
         pltpu.VMEM((PAIRS, ROWS, 128), BF16),
-        pltpu.VMEM((PAIRS, ROWS, 128), BF16),
-        pltpu.VMEM((PAIRS, ROWS, 256), BF16),
+        pltpu.VMEM((4, ROWS, 256), F32),
+        pltpu.VMEM((PAIRS, 2, SEQ_BITS * 64, 128), F32),
         pltpu.SemaphoreType.DMA((17,)),
         pltpu.SemaphoreType.DMA((12,)),
         pltpu.SemaphoreType.DMA((16,)),
@@ -408,21 +442,38 @@
         pltpu.SemaphoreType.DMA((N_SEM,)),
         pltpu.SemaphoreType.DMA((N_SEM,)),
     ]
-    return pl.pallas_call(
+    queries, keys, values, returned = pl.pallas_call(
         kernel,
         out_shape=(
-            jax.ShapeDtypeStruct((ROWS, HEADS * DK), BF16),
-            jax.ShapeDtypeStruct((ROWS, HEADS * DK), BF16),
-            jax.ShapeDtypeStruct((ROWS, HEADS * DV), BF16),
+            jax.ShapeDtypeStruct((PAIRS, ROWS, 128), BF16),
+            jax.ShapeDtypeStruct((PAIRS, ROWS, 128), F32),
+            jax.ShapeDtypeStruct((PAIRS, ROWS, 256), F32),
+            jax.ShapeDtypeStruct((ROWS, 128), BF16),
         ),
         in_specs=[any_space] * 5 + [vmem] * 2,
-        out_specs=(any_space,) * 3,
+        out_specs=(any_space,) * 3 + (vmem,),
         scratch_shapes=scratch,
         compiler_params=pltpu.CompilerParams(
             collective_id=0, has_side_effects=True, vmem_limit_bytes=56 * 1024 * 1024
         ),
         cost_estimate=pl.CostEstimate(flops=8_000_000_000, bytes_accessed=12_000_000, transcendentals=0),
     )(query_rows, key_rows, value_rows, out_grad, out_weight, level_codes, level_table)
+    narrow = pl.BlockSpec((ROWS, 128), lambda p: (0, p))
+    wide = pl.BlockSpec((ROWS, 256), lambda p: (0, p))
+    narrow_pair = pl.BlockSpec((1, ROWS, 128), lambda p: (p, 0, 0))
+    wide_pair = pl.BlockSpec((1, ROWS, 256), lambda p: (p, 0, 0))
+    return pl.pallas_call(
+        finish,
+        grid=(PAIRS,),
+        out_shape=(
+            jax.ShapeDtypeStruct((ROWS, HEADS * DK), BF16),
+            jax.ShapeDtypeStruct((ROWS, HEADS * DK), BF16),
+            jax.ShapeDtypeStruct((ROWS, HEADS * DV), BF16),
+        ),
+        in_specs=[pl.BlockSpec((128, 128), lambda p: (p, 0)), narrow, wide, narrow_pair, narrow_pair, wide_pair],
+        out_specs=(narrow, narrow, wide),
+        cost_estimate=pl.CostEstimate(flops=500_000_000, bytes_accessed=8_000_000, transcendentals=0),
+    )(returned, key_rows, value_rows, queries, keys, values)
 
 
 def solution(mesh):

time: 76.4 us -> 66.4 us (0.87)
  local copies, waits for them, and re-layouts: 6 us -> 0 us
  Pallas kernels: 69.5 us -> 65.5 us
    unnamed x3 -> x0, local copies, waits for them, and re-layouts: 6 us -> none
    pallas_call x1 -> x2, Pallas kernels: 69.5 us -> 65.5 us  [the longest x1 60.7 us: per_device(): pl.pallas_call(kernel, out_shape=(jax.ShapeDtypeStruct((PAIRS, ROWS, 128)...]
where the time goes in v2:
time: 66.4 us; the launch traced here: 66.2 us
  Pallas kernels  65.5 us (99%)
    pallas_call x1, Pallas kernels, per_device(): pl.pallas_call(kernel, out_shape=(jax.ShapeDtypeStruct((PAIRS, ROWS, 128)...  60.7 us
    pallas_call x1, Pallas kernels, per_device(): pl.pallas_call(finish, grid=(PAIRS,), out_shape=(jax.ShapeDtypeStruct((RO...  4.88 us

profile of v2, /device:TPU:1, one launch (start us, length us, event | category | flops | bytes accessed | tf_op | source)
XLA Modules:
  0.0 66.2 jit_solution(6973683566242187414)
XLA Ops:
  0.6 60.7 %shard_map.94 = (bf16[4,512,128]{2,1,0:T(8,128)(2,1)}, f32[4,512,128]{2,1,0:T(8,128)}, f32[4,512,256]{2,1,0:T(8,128)}, bf16[512,128]{1,0:T(8,128)(2,1)}) custom-call(bf16[512,512]{1,0:T(8,128)(2,1)} %q_hbm.1, bf16[512,512]{1,0:T(8,128)(2,1)} %k_ref.1, bf16[512,1024]{1,0:T(8,128)(2,1)} %v_ref.1, bf16[512,768]{1,0:T(8,128)(2,1)} %og_hbm.1, ...), custom_call_target="tpu_custom_call" | custom-call | flops 8000000000 | bytes 12000000 | tf_op jit(solution)/shard_map/pallas_call | solution.py:445
  61.3 4.9 %shard_map.95 = (bf16[512,512]{1,0:T(8,128)(2,1)}, bf16[512,512]{1,0:T(8,128)(2,1)}, bf16[512,1024]{1,0:T(8,128)(2,1)}) custom-call(bf16[512,128]{1,0:T(8,128)(2,1)} %get-tuple-element.7.ret_ref, bf16[512,512]{1,0:T(8,128)(2,1)} %k_ref.1, bf16[512,1024]{1,0:T(8,128)(2,1)} %v_ref.1, bf16[4,512,128]{2,1,0:T(8,128)(2,1)} %get-tuple-element.8.q_ref, ...), custom_call_target="tpu_custom_call" | custom-call | flops 500000000 | bytes 8000000 | tf_op jit(solution)/shard_map/pallas_call | solution.py:465

commit v3 on v2

--- a/solution.py
+++ b/solution.py
@@ -43,13 +43,13 @@
 
 
 def kernel(
-    q_hbm, k_hbm, v_hbm, og_hbm, w_hbm, codes_ref, table_ref,
-    qo_hbm, ko_hbm, vo_hbm, ret_ref,
-    qp, kp, vp, w4, gath, dout, kT, qT, lam, inner, sm,
+    q_hbm, k_hbm, v_hbm, og_hbm, w_hbm, codes_hbm, table_hbm,
+    qo, kacc, vacc, ret_ref, kp, vp,
+    qp, w4, gath, dout, kT, qT, lam, inner, sm,
     gsb, pgs, zbuf, xbuf, state_low,
     lg, rb0, rbh, rsrc, rbuf, tsrc, tbuf, rets, rfin,
-    kacc, vacc, qo, pacc, lgacc,
-    loc_sem, out_sem, ys, yr, ss, sr,
+    pacc, lgacc, codes_ref, table_ref,
+    loc_sem, ys, yr, ss, sr,
 ):
     g = lax.axis_index("seq")
     y = lax.axis_index("head")
@@ -75,6 +75,8 @@
         loads.append(pltpu.make_async_copy(v_hbm.at[:, pl.ds(p * 256, 256)], vp.at[p], loc_sem.at[len(loads)]))
     for p in range(PAIRS):
         loads.append(pltpu.make_async_copy(q_hbm.at[:, pl.ds(p * 128, 128)], qp.at[p], loc_sem.at[len(loads)]))
+    loads.append(pltpu.make_async_copy(codes_hbm, codes_ref, loc_sem.at[len(loads)]))
+    loads.append(pltpu.make_async_copy(table_hbm, table_ref, loc_sem.at[len(loads)]))
     loads.append(pltpu.make_async_copy(og_hbm, gath.at[y], loc_sem.at[len(loads)]))
     for p in range(4):
         loads.append(pltpu.make_async_copy(w_hbm.at[:, pl.ds(p * FEAT, FEAT)], w4.at[p], loc_sem.at[len(loads)]))
@@ -137,6 +139,8 @@
         start(owns[j])
     s0 = start([remote(gsb, pgs, ss, sr, S0, partner)])
 
+    for load in loads[8:14]:
+        load.wait()
     table = table_ref[...]
     columns = [jnp.broadcast_to(table[:, j:j + 1], (HEADS, ROWS)) for j in range(16)]
     for level in range(LB + 1 + SEQ_BITS):
@@ -155,9 +159,6 @@
             line = jnp.where(token_block == ct, lam[(ct ^ cs).bit_length()], line)
         inner[cs] = line
 
-    for load in loads[8:12]:
-        load.wait()
-
     def turned(p, _):
         qT[p] = qp[p].T
         return 0
@@ -241,7 +242,7 @@
                 lg[b, at, :] = grads[b * 64:(b + 1) * 64, :]
         return 0
 
-    for load in loads[12:]:
+    for load in loads[14:]:
         load.wait()
     project([y], 0, ROWS, True, False)
     turn(0)
@@ -342,21 +343,7 @@
         qo[p] = jnp.concatenate(lines, axis=0).T.astype(BF16)
         return 0
 
-    def store(p):
-        copies = [
-            pltpu.make_async_copy(qo.at[p], qo_hbm.at[p], out_sem.at[p]),
-            pltpu.make_async_copy(kacc.at[p], ko_hbm.at[p], out_sem.at[4 + p]),
-            pltpu.make_async_copy(vacc.at[p], vo_hbm.at[p], out_sem.at[8 + p]),
-        ]
-        for copy in copies:
-            copy.start()
-        outs.extend(copies)
-
-    outs = []
-
     lax.fori_loop(0, 2, attention, 0)
-    store(0)
-    store(1)
     arrive(r1x)
     tops = rbuf[0, pl.ds(3, 2)].astype(F32)
     for i in range(1, 8):
@@ -365,8 +352,6 @@
     r2 = start([remote(tsrc, tbuf.at[i], ss, sr, R2 + i - 1, x_peer(i)) for i in range(1, 4)])
 
     lax.fori_loop(2, 4, attention, 0)
-    store(2)
-    store(3)
     arrive(r1)
     arrive(r2)
     outer = tbuf[1, 0].astype(F32) + tbuf[2, 1].astype(F32) + tbuf[3, 1].astype(F32)
@@ -381,24 +366,34 @@
     arrive(rb)
     arrive(r3)
     r4 = start([remote(rfin.at[mine], rfin.at[mine], ss, sr, R4, partner)])
-    for copy in outs:
-        copy.wait()
     arrive(r4)
     ret_ref[...] = (rfin[...].astype(F32) + rb0[...].astype(F32)).astype(BF16)
     for copy in sent:
         copy.wait_send()
 
 
-def finish(ret_ref, k_ref, v_ref, q_ref, kacc_ref, vacc_ref, qo_ref, ko_ref, vo_ref):
-    back = ret_ref[...]
+def finish(back_ref, k_ref, v_ref, q_ref, kacc_ref, vacc_ref, qo_hbm, ko_hbm, vo_hbm, ko, vo, sem):
+    copies = []
+
+    def send(src, dst):
+        copies.append(pltpu.make_async_copy(src, dst, sem.at[len(copies)]))
+        copies[-1].start()
+
+    for p in range(PAIRS):
+        send(q_ref.at[p], qo_hbm.at[:, pl.ds(p * 128, 128)])
     zero = jnp.zeros((64, 128), BF16)
-    spread = jnp.concatenate([
-        jnp.concatenate([back[:64], zero], axis=1),
-        jnp.concatenate([zero, back[64:]], axis=1),
-    ], axis=0)
-    qo_ref[...] = q_ref[0]
-    ko_ref[...] = (kacc_ref[0] + nt(v_ref[...], spread)).astype(BF16)
-    vo_ref[...] = (vacc_ref[0] + nn(k_ref[...], spread)).astype(BF16)
+    for p in range(PAIRS):
+        back = back_ref[pl.ds(p * 128, 128), :]
+        spread = jnp.concatenate([
+            jnp.concatenate([back[:64], zero], axis=1),
+            jnp.concatenate([zero, back[64:]], axis=1),
+        ], axis=0)
+        vo[p] = (vacc_ref[p] + nn(k_ref[p], spread)).astype(BF16)
+        send(vo.at[p], vo_hbm.at[:, pl.ds(p * 256, 256)])
+        ko[p] = (kacc_ref[p] + nt(v_ref[p], spread)).astype(BF16)
+        send(ko.at[p], ko_hbm.at[:, pl.ds(p * 128, 128)])
+    for copy in copies:
+        copy.wait()
 
 
 def per_device(query_rows, key_rows, value_rows, out_grad, out_weight, level_codes, level_table):
@@ -406,8 +401,6 @@
     vmem = pl.BlockSpec(memory_space=pltpu.VMEM)
     scratch = [
         pltpu.VMEM((PAIRS, ROWS, 128), BF16),
-        pltpu.VMEM((PAIRS, ROWS, 128), BF16),
-        pltpu.VMEM((PAIRS, ROWS, 256), BF16),
         pltpu.VMEM((4, HEADS * DV, FEAT), BF16),
         pltpu.VMEM((4, ROWS, FEAT), BF16),
         pltpu.VMEM((HEADS, ROWS, DV), BF16),
@@ -430,50 +423,55 @@
         pltpu.VMEM((4, 2, SLICE, 128), BF16),
         pltpu.VMEM((8, SLICE, 128), BF16),
         pltpu.VMEM((ROWS, 128), BF16),
-        pltpu.VMEM((PAIRS, ROWS, 128), F32),
-        pltpu.VMEM((PAIRS, ROWS, 256), F32),
-        pltpu.VMEM((PAIRS, ROWS, 128), BF16),
         pltpu.VMEM((4, ROWS, 256), F32),
         pltpu.VMEM((PAIRS, 2, SEQ_BITS * 64, 128), F32),
-        pltpu.SemaphoreType.DMA((17,)),
-        pltpu.SemaphoreType.DMA((12,)),
+        pltpu.VMEM((12, HEADS, ROWS), jnp.int32),
+        pltpu.VMEM((HEADS, 16), F32),
+        pltpu.SemaphoreType.DMA((19,)),
         pltpu.SemaphoreType.DMA((16,)),
         pltpu.SemaphoreType.DMA((16,)),
         pltpu.SemaphoreType.DMA((N_SEM,)),
         pltpu.SemaphoreType.DMA((N_SEM,)),
     ]
-    queries, keys, values, returned = pl.pallas_call(
+    inputs = [
+        pltpu.with_memory_space_constraint(array, pltpu.HBM)
+        for array in (query_rows, key_rows, value_rows, out_grad, out_weight, level_codes, level_table)
+    ]
+    queries, keys, values, returned, key_pairs, value_pairs = pl.pallas_call(
         kernel,
         out_shape=(
-            jax.ShapeDtypeStruct((PAIRS, ROWS, 128), BF16),
-            jax.ShapeDtypeStruct((PAIRS, ROWS, 128), F32),
-            jax.ShapeDtypeStruct((PAIRS, ROWS, 256), F32),
-            jax.ShapeDtypeStruct((ROWS, 128), BF16),
+            pltpu.VMEM((PAIRS, ROWS, 128), BF16),
+            pltpu.VMEM((PAIRS, ROWS, 128), F32),
+            pltpu.VMEM((PAIRS, ROWS, 256), F32),
+            pltpu.VMEM((ROWS, 128), BF16),
+            pltpu.VMEM((PAIRS, ROWS, 128), BF16),
+            pltpu.VMEM((PAIRS, ROWS, 256), BF16),
         ),
-        in_specs=[any_space] * 5 + [vmem] * 2,
-        out_specs=(any_space,) * 3 + (vmem,),
+        in_specs=[any_space] * 7,
+        out_specs=(vmem,) * 6,
         scratch_shapes=scratch,
         compiler_params=pltpu.CompilerParams(
-            collective_id=0, has_side_effects=True, vmem_limit_bytes=56 * 1024 * 1024
+            collective_id=0, has_side_effects=True, vmem_limit_bytes=40 * 1024 * 1024
         ),
         cost_estimate=pl.CostEstimate(flops=8_000_000_000, bytes_accessed=12_000_000, transcendentals=0),
-    )(query_rows, key_rows, value_rows, out_grad, out_weight, level_codes, level_table)
-    narrow = pl.BlockSpec((ROWS, 128), lambda p: (0, p))
-    wide = pl.BlockSpec((ROWS, 256), lambda p: (0, p))
-    narrow_pair = pl.BlockSpec((1, ROWS, 128), lambda p: (p, 0, 0))
-    wide_pair = pl.BlockSpec((1, ROWS, 256), lambda p: (p, 0, 0))
+    )(*inputs)
     return pl.pallas_call(
         finish,
-        grid=(PAIRS,),
         out_shape=(
             jax.ShapeDtypeStruct((ROWS, HEADS * DK), BF16),
             jax.ShapeDtypeStruct((ROWS, HEADS * DK), BF16),
             jax.ShapeDtypeStruct((ROWS, HEADS * DV), BF16),
         ),
-        in_specs=[pl.BlockSpec((128, 128), lambda p: (p, 0)), narrow, wide, narrow_pair, narrow_pair, wide_pair],
-        out_specs=(narrow, narrow, wide),
+        in_specs=[vmem] * 6,
+        out_specs=(any_space,) * 3,
+        scratch_shapes=[
+            pltpu.VMEM((PAIRS, ROWS, 128), BF16),
+            pltpu.VMEM((PAIRS, ROWS, 256), BF16),
+            pltpu.SemaphoreType.DMA((3 * PAIRS,)),
+        ],
+        compiler_params=pltpu.CompilerParams(vmem_limit_bytes=16 * 1024 * 1024),
         cost_estimate=pl.CostEstimate(flops=500_000_000, bytes_accessed=8_000_000, transcendentals=0),
-    )(returned, key_rows, value_rows, queries, keys, values)
+    )(returned, key_pairs, value_pairs, queries, keys, values)
 
 
 def solution(mesh):

time: 66.4 us -> 61.7 us (0.929)
  Pallas kernels: 65.5 us -> 61 us
    pallas_call x2, Pallas kernels: 65.5 us -> 61 us  [the longest x1 59.4 us: per_device(): pl.pallas_call(kernel, out_shape=(pltpu.VMEM((PAIRS, ROWS, 128), BF16), p...]
where the time goes in v3:
time: 61.7 us; the launch traced here: 61.6 us
  Pallas kernels  61 us (99%)
  between operations  0.64 us (1%)
    pallas_call x1, Pallas kernels, per_device(): pl.pallas_call(kernel, out_shape=(pltpu.VMEM((PAIRS, ROWS, 128), BF16), p...  59.4 us
    pallas_call x1, Pallas kernels, per_device(): pl.pallas_call(finish, out_shape=(jax.ShapeDtypeStruct((ROWS, HEADS * DK)...  1.53 us

profile of v3, /device:TPU:1, one launch (start us, length us, event | category | flops | bytes accessed | tf_op | source)
XLA Modules:
  0.0 61.6 jit_solution(13156162699607146123)
XLA Ops:
  0.6 59.4 %shard_map.94 = (bf16[4,512,128]{2,1,0:T(8,128)(2,1)S(1)}, f32[4,512,128]{2,1,0:T(8,128)S(1)}, f32[4,512,256]{2,1,0:T(8,128)S(1)}, bf16[512,128]{1,0:T(8,128)(2,...) custom-call(bf16[512,512]{1,0:T(8,128)(2,1)} %q_hbm.1, bf16[512,512]{1,0:T(8,128)(2,1)} %k_hbm.1, ...), custom_call_target="tpu_custom_call" | custom-call | flops 8000000000 | bytes 12000000 | tf_op jit(solution)/shard_map/pallas_call | solution.py:440
  60.1 1.5 %shard_map.95 = (bf16[512,512]{1,0:T(8,128)(2,1)}, bf16[512,512]{1,0:T(8,128)(2,1)}, bf16[512,1024]{1,0:T(8,128)(2,1)}) custom-call(bf16[512,128]{1,0:T(8,128)(2,1)S(1)} %get-tuple-element.9.back_ref, bf16[4,512,128]{2,1,0:T(8,128)(2,1)S(1)} %get-tuple-element.10.k_ref, bf16[4,512,256]{2,1,0:T(8,128)(2,1)S(1)} %get-tuple-element.11.v_ref, ...), custom_call_target="tpu_custom_call" | custom-call | flops 500000000 | bytes 8000000 | tf_op jit(solution)/shard_map/pallas_call | solution.py:458

commit v4 on v3

--- a/solution.py
+++ b/solution.py
@@ -23,7 +23,8 @@
 F32 = jnp.float32
 BF16 = jnp.bfloat16
 
-S0, S1, S2, S4, R0, R1, R2, R3, R4, N_SEM = 0, 1, 8, 11, 16, 27, 41, 44, 51, 52
+S0, S1, S2, S4, R0, R1, R2, R3, N_SEM = 0, 1, 8, 11, 16, 27, 67, 70, 86
+FAR_FIRST = (4, 5, 3, 7, 6, 2, 1)
 
 
 def nt(a, b):
@@ -61,12 +62,17 @@
     def z_peer(i):
         return (x * 16 + flipped(z, i, 3) * 2 + c, y)
 
+    def z_other(i):
+        return (x * 16 + flipped(z, i, 3) * 2 + 1 - c, y)
+
     def x_peer(i):
         return (flipped(x, i, 2) * 16 + z * 2 + c, y)
 
     partner = (g + 1 - 2 * c, y)
-    peers = [partner, (g, right), (g, left)]
-    peers += [z_peer(i) for i in range(1, 8)] + [x_peer(i) for i in range(1, 4)]
+    def z_ring(step):
+        return (x * 16 + ((z + step) % 8) * 2 + c, y)
+
+    peers = [partner, (g, right), (g, left), z_ring(1), z_ring(7), x_peer(1), x_peer(3)]
 
     loads = []
     for p in range(PAIRS):
@@ -83,10 +89,64 @@
     for load in loads:
         load.start()
 
+    rbuf[...] = jnp.zeros_like(rbuf)
+    tbuf[...] = jnp.zeros_like(tbuf)
+
     barrier = pltpu.get_barrier_semaphore()
     for peer in peers:
         pl.semaphore_signal(barrier, inc=1, device_id=peer, device_id_type=pl.DeviceIdType.MESH)
 
+    pl.semaphore_wait(barrier, len(peers))
+
+    def remote(src, dst, send, recv, slot, to):
+        return pltpu.make_async_remote_copy(
+            src_ref=src, dst_ref=dst, send_sem=send.at[slot], recv_sem=recv.at[slot],
+            device_id=to, device_id_type=pl.DeviceIdType.MESH,
+        )
+
+    def own(j):
+        rows = pl.ds(j * CROWS, CROWS)
+        return [
+            remote(og_hbm.at[rows], gath.at[y, rows], ys, yr, j, (g, right)),
+            remote(og_hbm.at[rows], gath.at[y, rows], ys, yr, 4 + j, (g, left)),
+        ]
+
+    def forward(j):
+        first = pl.ds(j * CROWS, CROWS // 2)
+        second = pl.ds(j * CROWS + CROWS // 2, CROWS // 2)
+        return [
+            remote(gath.at[left, first], gath.at[left, first], ys, yr, 8 + j, (g, right)),
+            remote(gath.at[right, second], gath.at[right, second], ys, yr, 12 + j, (g, left)),
+        ]
+
+    def start(copies):
+        for copy in copies:
+            copy.start()
+        sent.extend(copies)
+        return copies
+
+    def arrive(copies):
+        for copy in copies:
+            copy.wait_recv()
+
+    def start_if(condition, copies):
+        @pl.when(condition)
+        def _():
+            for copy in copies:
+                copy.start()
+
+        sent_if.append((condition, copies))
+
+    def arrive_if(condition, copies):
+        @pl.when(condition)
+        def _():
+            arrive(copies)
+
+    sent, sent_if = [], []
+    owns = [own(j) for j in range(CHUNKS)]
+    forwards = [forward(j) for j in range(CHUNKS)]
+    for j in range(CHUNKS):
+        start(owns[j])
     for load in loads[:8]:
         load.wait()
 
@@ -99,44 +159,6 @@
         return 0
 
     lax.fori_loop(0, PAIRS, states_of, 0)
-    pl.semaphore_wait(barrier, len(peers))
-
-    def remote(src, dst, send, recv, slot, to):
-        return pltpu.make_async_remote_copy(
-            src_ref=src, dst_ref=dst, send_sem=send.at[slot], recv_sem=recv.at[slot],
-            device_id=to, device_id_type=pl.DeviceIdType.MESH,
-        )
-
-    def own(j):
-        rows = pl.ds(j * CROWS, CROWS)
-        return [
-            remote(og_hbm.at[rows], gath.at[y, rows], ys, yr, j, (g, right)),
-            remote(og_hbm.at[rows], gath.at[y, rows], ys, yr, 4 + j, (g, left)),
-        ]
-
-    def forward(j):
-        first = pl.ds(j * CROWS, CROWS // 2)
-        second = pl.ds(j * CROWS + CROWS // 2, CROWS // 2)
-        return [
-            remote(gath.at[left, first], gath.at[left, first], ys, yr, 8 + j, (g, right)),
-            remote(gath.at[right, second], gath.at[right, second], ys, yr, 12 + j, (g, left)),
-        ]
-
-    def start(copies):
-        for copy in copies:
-            copy.start()
-        sent.extend(copies)
-        return copies
-
-    def arrive(copies):
-        for copy in copies:
-            copy.wait_recv()
-
-    sent = []
-    owns = [own(j) for j in range(CHUNKS)]
-    forwards = [forward(j) for j in range(CHUNKS)]
-    for j in range(CHUNKS):
-        start(owns[j])
     s0 = start([remote(gsb, pgs, ss, sr, S0, partner)])
 
     for load in loads[8:14]:
@@ -168,8 +190,17 @@
     mine = pl.ds(pl.multiple_of(c * HALF, HALF), HALF)
     other = pl.ds(pl.multiple_of((1 - c) * HALF, HALF), HALF)
     arrive(s0)
-    zbuf[0] = (gsb[mine, :] + pgs[mine, :]).astype(BF16)
-    s1 = start([remote(zbuf.at[0], zbuf.at[i], ss, sr, S1 + i - 1, z_peer(i)) for i in range(1, 8)])
+    zbuf[z] = (gsb[mine, :] + pgs[mine, :]).astype(BF16)
+
+    def ring(k):
+        ahead, back = zbuf.at[(z + 8 - k) % 8], zbuf.at[(z + k) % 8]
+        copies = [remote(ahead, ahead, ss, sr, S1 + k, z_ring(1))]
+        if k < 3:
+            copies.append(remote(back, back, ss, sr, S1 + 4 + k, z_ring(7)))
+        return copies
+
+    s1 = [ring(k) for k in range(4)]
+    start(s1[0])
     state_low[0] = pgs[...].astype(BF16)
 
     def turn(j):
@@ -221,46 +252,58 @@
 
         lax.fori_loop(0, 4, tile, 0)
 
-    def level_part(p, e, first):
+    def level_part(p, e, first, count):
         h = 2 * p + e
-        rows = qT[p, e * 64:(e + 1) * 64, first:first + HALF].astype(F32)
+        rows = qT[p, e * 64:(e + 1) * 64, first:first + count].astype(F32)
         scaled = [
-            (lam[LB + 1 + b, pl.ds(h, 1), first:first + HALF] * rows).astype(BF16) for b in range(SEQ_BITS)
+            (lam[LB + 1 + b, pl.ds(h, 1), :][:, first:first + count] * rows).astype(BF16) for b in range(SEQ_BITS)
         ]
-        return nn(jnp.concatenate(scaled, axis=0), dout[h, first:first + HALF, :])
+        return nn(jnp.concatenate(scaled, axis=0), dout[h, first:first + count, :])
 
     def level_first(p, _):
         for e in range(2):
-            lgacc[p, e] = level_part(p, e, 0)
+            lgacc[p, e] = level_part(p, e, 0, HALF)
         return 0
 
-    def level_rest(p, _):
+    def level_next(p, _):
         for e in range(2):
-            grads = (lgacc[p, e] + level_part(p, e, HALF)).astype(BF16)
+            lgacc[p, e] += level_part(p, e, HALF, CROWS)
+        return 0
+
+    def level_last(p):
+        for e in range(2):
+            grads = (lgacc[p, e] + level_part(p, e, HALF + CROWS, CROWS)).astype(BF16)
             at = pl.ds(pl.multiple_of(p * 128 + e * 64, 64), 64)
             for b in range(SEQ_BITS):
                 lg[b, at, :] = grads[b * 64:(b + 1) * 64, :]
-        return 0
 
     for load in loads[14:]:
         load.wait()
     project([y], 0, ROWS, True, False)
+    arrive(s1[0])
+    start(s1[1])
     turn(0)
+    arrive(s1[1])
+    start(s1[2])
     turn(1)
     project([left, right], 0, HALF, False, False)
+    arrive(s1[2])
+    start(s1[3])
     turn(2)
-    turn(3)
-
-    arrive(s1)
-    parts = [zbuf[i].astype(F32) for i in range(8)]
+
+    arrive(s1[3])
+    parts = [zbuf[flipped(z, i, 3)].astype(F32) for i in range(8)]
     pair1 = parts[2] + parts[3]
     quad = (parts[4] + parts[5]) + (parts[6] + parts[7])
     xbuf[0] = ((parts[0] + parts[1]) + pair1 + quad).astype(BF16)
-    s2 = start([remote(xbuf.at[0], xbuf.at[i], ss, sr, S2 + i - 1, x_peer(i)) for i in range(1, 4)])
-    state_low[1, mine, :] = zbuf[1]
+    s2 = start([remote(xbuf.at[0], xbuf.at[i], ss, sr, S2 + i - 1, x_peer(i)) for i in (1, 3)])
+    state_low[1, mine, :] = parts[1].astype(BF16)
     state_low[2, mine, :] = pair1.astype(BF16)
     state_low[3, mine, :] = quad.astype(BF16)
 
+    turn(3)
+    arrive(s2)
+    s2 = start([remote(xbuf.at[1], xbuf.at[2], ss, sr, S2 + 1, x_peer(3))])
     project([left, right], HALF, HALF, False, False)
     arrive(forwards[0])
     arrive(forwards[1])
@@ -275,34 +318,40 @@
     ])
 
     arrive(forwards[2])
+    project([across], HALF, CROWS, False, True)
+    lax.fori_loop(0, PAIRS, level_next, 0)
     arrive(forwards[3])
-    project([across], HALF, HALF, False, True)
+    project([across], HALF + CROWS, CROWS, False, True)
 
     r0 = []
     for i in range(2):
         p = 2 * (1 - c) + i
-        level_rest(p, 0)
+        level_last(p)
         rows = pl.ds(pl.multiple_of(p * 128, 128), 128)
         r0 += start([
             remote(lg.at[1 + b, rows], rbh.at[b, pl.ds(i * 128, 128)], ss, sr, R0 + 5 * i + b, partner)
             for b in range(5)
         ])
     for i in range(2):
-        level_rest(2 * c + i, 0)
+        level_last(2 * c + i)
     arrive(r0)
     rsrc[...] = (lg[pl.ds(1, 5), mine, :].astype(F32) + rbh[...].astype(F32)).astype(BF16)
 
     def owned(at):
         return pl.ds(pl.multiple_of(at * SLICE, SLICE), SLICE)
 
-    r1x = start([
-        remote(rsrc.at[pl.ds(3, 2), owned(flipped(z, i, 3))], rbuf.at[i, pl.ds(3, 2)], ss, sr, R1 + i - 1, z_peer(i))
-        for i in range(1, 8)
-    ])
-    r1 = start([
-        remote(rsrc.at[pl.ds(0, 3), owned(flipped(z, i, 3))], rbuf.at[i, pl.ds(0, 3)], ss, sr, R1 + 6 + i, z_peer(i))
-        for i in range(1, 8)
-    ])
+    def slice_of(i, level):
+        return remote(
+            rsrc.at[level, owned(flipped(z, i, 3))], rbuf.at[i, level], ss, sr, R1 + 8 * level + i, z_peer(i)
+        )
+
+    upper = [x % 2 == 1, x // 2 == 1]
+    for i in FAR_FIRST:
+        for b in range(2):
+            start_if(upper[b], [slice_of(i, 3 + b)])
+    for i in FAR_FIRST:
+        for b in range(3):
+            start_if((z // 2**b) % 2 == 1, [slice_of(i, b)])
     rbuf[0] = rsrc[:, owned(z), :]
     rb = start([remote(lg.at[0], rb0, ss, sr, R0 + 10, partner)])
     arrive(s4)
@@ -344,16 +393,23 @@
         return 0
 
     lax.fori_loop(0, 2, attention, 0)
-    arrive(r1x)
+    for b in range(2):
+        arrive_if(upper[b], [slice_of(i, 3 + b) for i in FAR_FIRST])
     tops = rbuf[0, pl.ds(3, 2)].astype(F32)
     for i in range(1, 8):
         tops = tops + rbuf[i, pl.ds(3, 2)].astype(F32)
     tsrc[...] = tops.astype(BF16)
-    r2 = start([remote(tsrc, tbuf.at[i], ss, sr, R2 + i - 1, x_peer(i)) for i in range(1, 4)])
+    near = [remote(tsrc.at[0], tbuf.at[1, 0], ss, sr, R2, x_peer(1))]
+    far = [remote(tsrc.at[1], tbuf.at[i, 1], ss, sr, R2 + i - 1, x_peer(i)) for i in (2, 3)]
+    start_if(upper[1], far)
+    start_if(upper[0], near)
 
     lax.fori_loop(2, 4, attention, 0)
-    arrive(r1)
-    arrive(r2)
+    for i in FAR_FIRST:
+        for b in range(3):
+            arrive_if((flipped(z, i, 3) // 2**b) % 2 == 1, [slice_of(i, b)])
+    arrive_if(x % 2 == 0, near)
+    arrive_if(x // 2 == 0, far)
     outer = tbuf[1, 0].astype(F32) + tbuf[2, 1].astype(F32) + tbuf[3, 1].astype(F32)
     for r in range(8):
         total = outer
@@ -361,15 +417,24 @@
             total = total + rbuf[r ^ i, i.bit_length() - 1].astype(F32)
         rets[r] = total.astype(BF16)
     finals = pl.ds(pl.multiple_of(c * HALF + z * SLICE, SLICE), SLICE)
-    r3 = start([remote(rets.at[i], rfin.at[finals], ss, sr, R3 + i - 1, z_peer(i)) for i in range(1, 8)])
+    r3 = []
+    for i in FAR_FIRST:
+        r3 += start([
+            remote(rets.at[i], rfin.at[finals], ss, sr, R3 + i, z_peer(i)),
+            remote(rets.at[i], rfin.at[finals], ss, sr, R3 + 8 + i, z_other(i)),
+        ])
+    r3 += start([remote(rets.at[0], rfin.at[finals], ss, sr, R3 + 8, partner)])
     rfin[finals, :] = rets[0]
     arrive(rb)
     arrive(r3)
-    r4 = start([remote(rfin.at[mine], rfin.at[mine], ss, sr, R4, partner)])
-    arrive(r4)
     ret_ref[...] = (rfin[...].astype(F32) + rb0[...].astype(F32)).astype(BF16)
     for copy in sent:
         copy.wait_send()
+    for condition, copies in sent_if:
+        @pl.when(condition)
+        def _(copies=copies):
+            for copy in copies:
+                copy.wait_send()
 
 
 def finish(back_ref, k_ref, v_ref, q_ref, kacc_ref, vacc_ref, qo_hbm, ko_hbm, vo_hbm, ko, vo, sem):

time: 61.7 us -> 59 us (0.956)
  Pallas kernels: 61 us -> 58.2 us
    pallas_call x1, Pallas kernels: 59.4 us -> 56.7 us  [per_device(): pl.pallas_call(kernel, out_shape=(pltpu.VMEM((PAIRS, ROWS, 128), BF16), p...]
where the time goes in v4:
time: 59 us; the launch traced here: 58.9 us
  Pallas kernels  58.2 us (99%)
  between operations  0.64 us (1%)
    pallas_call x1, Pallas kernels, per_device(): pl.pallas_call(kernel, out_shape=(pltpu.VMEM((PAIRS, ROWS, 128), BF16), p...  56.7 us
    pallas_call x1, Pallas kernels, per_device(): pl.pallas_call(finish, out_shape=(jax.ShapeDtypeStruct((ROWS, HEADS * DK)...  1.53 us

profile of v4, /device:TPU:1, one launch (start us, length us, event | category | flops | bytes accessed | tf_op | source)
XLA Modules:
  0.0 58.9 jit_solution(15362053374177528590)
XLA Ops:
  0.6 56.7 %shard_map.94 = (bf16[4,512,128]{2,1,0:T(8,128)(2,1)S(1)}, f32[4,512,128]{2,1,0:T(8,128)S(1)}, f32[4,512,256]{2,1,0:T(8,128)S(1)}, bf16[512,128]{1,0:T(8,128)(2,...) custom-call(bf16[512,512]{1,0:T(8,128)(2,1)} %q_hbm.1, bf16[512,512]{1,0:T(8,128)(2,1)} %k_hbm.1, ...), custom_call_target="tpu_custom_call" | custom-call | flops 8000000000 | bytes 12000000 | tf_op jit(solution)/shard_map/pallas_call | solution.py:505
  57.4 1.5 %shard_map.95 = (bf16[512,512]{1,0:T(8,128)(2,1)}, bf16[512,512]{1,0:T(8,128)(2,1)}, bf16[512,1024]{1,0:T(8,128)(2,1)}) custom-call(bf16[512,128]{1,0:T(8,128)(2,1)S(1)} %get-tuple-element.9.back_ref, bf16[4,512,128]{2,1,0:T(8,128)(2,1)S(1)} %get-tuple-element.10.k_ref, bf16[4,512,256]{2,1,0:T(8,128)(2,1)S(1)} %get-tuple-element.11.v_ref, ...), custom_call_target="tpu_custom_call" | custom-call | flops 500000000 | bytes 8000000 | tf_op jit(solution)/shard_map/pallas_call | solution.py:523

commit v5 on v4

--- a/solution.py
+++ b/solution.py
@@ -74,6 +74,10 @@
 
     peers = [partner, (g, right), (g, left), z_ring(1), z_ring(7), x_peer(1), x_peer(3)]
 
+    barrier = pltpu.get_barrier_semaphore()
+    for peer in peers:
+        pl.semaphore_signal(barrier, inc=1, device_id=peer, device_id_type=pl.DeviceIdType.MESH)
+
     loads = []
     for p in range(PAIRS):
         loads.append(pltpu.make_async_copy(k_hbm.at[:, pl.ds(p * 128, 128)], kp.at[p], loc_sem.at[len(loads)]))
@@ -86,16 +90,6 @@
     loads.append(pltpu.make_async_copy(og_hbm, gath.at[y], loc_sem.at[len(loads)]))
     for p in range(4):
         loads.append(pltpu.make_async_copy(w_hbm.at[:, pl.ds(p * FEAT, FEAT)], w4.at[p], loc_sem.at[len(loads)]))
-    for load in loads:
-        load.start()
-
-    rbuf[...] = jnp.zeros_like(rbuf)
-    tbuf[...] = jnp.zeros_like(tbuf)
-
-    barrier = pltpu.get_barrier_semaphore()
-    for peer in peers:
-        pl.semaphore_signal(barrier, inc=1, device_id=peer, device_id_type=pl.DeviceIdType.MESH)
-
     pl.semaphore_wait(barrier, len(peers))
 
     def remote(src, dst, send, recv, slot, to):
@@ -147,6 +141,10 @@
     forwards = [forward(j) for j in range(CHUNKS)]
     for j in range(CHUNKS):
         start(owns[j])
+    for load in loads:
+        load.start()
+    rbuf[...] = jnp.zeros_like(rbuf)
+    tbuf[...] = jnp.zeros_like(tbuf)
     for load in loads[:8]:
         load.wait()
 
@@ -234,23 +232,23 @@
 
     lax.fori_loop(0, PAIRS, scores_of, 0)
 
-    def project(slots, first, count, begin, end):
-        def tile(n, _):
-            cols = pl.ds(pl.multiple_of(n * 256, 256), 256)
-            rows = pl.ds(first, count)
-            total = None if begin else pacc[n, rows, :]
-            for d in slots:
-                part = nt(gath[d, rows, :], w4[d, cols, :])
-                total = part if total is None else total + part
-            if end:
-                low = total.astype(BF16)
-                dout[2 * n, rows, :] = low[:, :128]
-                dout[2 * n + 1, rows, :] = low[:, 128:]
-            else:
-                pacc[n, rows, :] = total
-            return 0
-
-        lax.fori_loop(0, 4, tile, 0)
+    def project_pair(n, slots, first, count, begin, end):
+        cols = pl.ds(pl.multiple_of(n * 256, 256), 256)
+        rows = pl.ds(first, count)
+        total = None if begin else pacc[n, rows, :]
+        for d in slots:
+            part = nt(gath[d, rows, :], w4[d, cols, :])
+            total = part if total is None else total + part
+        if end:
+            low = total.astype(BF16)
+            dout[2 * n, rows, :] = low[:, :128]
+            dout[2 * n + 1, rows, :] = low[:, 128:]
+        else:
+            pacc[n, rows, :] = total
+
+    def project(*how):
+        for n in range(PAIRS):
+            project_pair(n, *how)
 
     def level_part(p, e, first, count):
         h = 2 * p + e
@@ -265,14 +263,9 @@
             lgacc[p, e] = level_part(p, e, 0, HALF)
         return 0
 
-    def level_next(p, _):
-        for e in range(2):
-            lgacc[p, e] += level_part(p, e, HALF, CROWS)
-        return 0
-
     def level_last(p):
         for e in range(2):
-            grads = (lgacc[p, e] + level_part(p, e, HALF + CROWS, CROWS)).astype(BF16)
+            grads = (lgacc[p, e] + level_part(p, e, HALF, HALF)).astype(BF16)
             at = pl.ds(pl.multiple_of(p * 128 + e * 64, 64), 64)
             for b in range(SEQ_BITS):
                 lg[b, at, :] = grads[b * 64:(b + 1) * 64, :]
@@ -308,18 +301,10 @@
     arrive(forwards[0])
     arrive(forwards[1])
     project([across], 0, HALF, False, True)
-    lax.fori_loop(0, PAIRS, level_first, 0)
-
-    arrive(s2)
-    state_low[4, mine, :] = xbuf[1]
-    state_low[5, mine, :] = (xbuf[2].astype(F32) + xbuf[3].astype(F32)).astype(BF16)
-    s4 = start([
-        remote(state_low.at[b, mine], state_low.at[b, mine], ss, sr, S4 + b - 1, partner) for b in range(1, SEQ_BITS)
-    ])
+    lax.fori_loop(0, PAIRS, level_first, 0, unroll=True)
 
     arrive(forwards[2])
     project([across], HALF, CROWS, False, True)
-    lax.fori_loop(0, PAIRS, level_next, 0)
     arrive(forwards[3])
     project([across], HALF + CROWS, CROWS, False, True)
 
@@ -354,6 +339,12 @@
             start_if((z // 2**b) % 2 == 1, [slice_of(i, b)])
     rbuf[0] = rsrc[:, owned(z), :]
     rb = start([remote(lg.at[0], rb0, ss, sr, R0 + 10, partner)])
+    arrive(s2)
+    state_low[4, mine, :] = xbuf[1]
+    state_low[5, mine, :] = (xbuf[2].astype(F32) + xbuf[3].astype(F32)).astype(BF16)
+    s4 = start([
+        remote(state_low.at[b, mine], state_low.at[b, mine], ss, sr, S4 + b - 1, partner) for b in range(1, SEQ_BITS)
+    ])
     arrive(s4)
 
     def attention(p, _):
@@ -411,19 +402,16 @@
     arrive_if(x % 2 == 0, near)
     arrive_if(x // 2 == 0, far)
     outer = tbuf[1, 0].astype(F32) + tbuf[2, 1].astype(F32) + tbuf[3, 1].astype(F32)
-    for r in range(8):
+    finals = pl.ds(pl.multiple_of(c * HALF + z * SLICE, SLICE), SLICE)
+    r3 = []
+    for r in FAR_FIRST + (0,):
         total = outer
         for i in range(1, 8):
             total = total + rbuf[r ^ i, i.bit_length() - 1].astype(F32)
         rets[r] = total.astype(BF16)
-    finals = pl.ds(pl.multiple_of(c * HALF + z * SLICE, SLICE), SLICE)
-    r3 = []
-    for i in FAR_FIRST:
-        r3 += start([
-            remote(rets.at[i], rfin.at[finals], ss, sr, R3 + i, z_peer(i)),
-            remote(rets.at[i], rfin.at[finals], ss, sr, R3 + 8 + i, z_other(i)),
-        ])
-    r3 += start([remote(rets.at[0], rfin.at[finals], ss, sr, R3 + 8, partner)])
+        if r:
+            r3 += start([remote(rets.at[r], rfin.at[finals], ss, sr, R3 + r, z_peer(r))])
+        r3 += start([remote(rets.at[r], rfin.at[finals], ss, sr, R3 + 8 + r, z_other(r) if r else partner)])
     rfin[finals, :] = rets[0]
     arrive(rb)
     arrive(r3)

time: 59 us -> 57.3 us (0.971)
  Pallas kernels: 58.2 us -> 56.5 us
    pallas_call x1, Pallas kernels: 56.7 us -> 55 us  [per_device(): pl.pallas_call(kernel, out_shape=(pltpu.VMEM((PAIRS, ROWS, 128), BF16), p...]
where the time goes in v5:
time: 57.3 us; the launch traced here: 57.2 us
  Pallas kernels  56.5 us (99%)
  between operations  0.64 us (1%)
    pallas_call x1, Pallas kernels, per_device(): pl.pallas_call(kernel, out_shape=(pltpu.VMEM((PAIRS, ROWS, 128), BF16), p...  55 us
    pallas_call x1, Pallas kernels, per_device(): pl.pallas_call(finish, out_shape=(jax.ShapeDtypeStruct((ROWS, HEADS * DK)...  1.53 us

profile of v5, /device:TPU:1, one launch (start us, length us, event | category | flops | bytes accessed | tf_op | source)
XLA Modules:
  0.0 57.2 jit_solution(10711936664615273328)
XLA Ops:
  0.6 55.0 %shard_map.94 = (bf16[4,512,128]{2,1,0:T(8,128)(2,1)S(1)}, f32[4,512,128]{2,1,0:T(8,128)S(1)}, f32[4,512,256]{2,1,0:T(8,128)S(1)}, bf16[512,128]{1,0:T(8,128)(2,...) custom-call(bf16[512,512]{1,0:T(8,128)(2,1)} %q_hbm.1, bf16[512,512]{1,0:T(8,128)(2,1)} %k_hbm.1, ...), custom_call_target="tpu_custom_call" | custom-call | flops 8000000000 | bytes 12000000 | tf_op jit(solution)/shard_map/pallas_call | solution.py:493
  55.6 1.5 %shard_map.95 = (bf16[512,512]{1,0:T(8,128)(2,1)}, bf16[512,512]{1,0:T(8,128)(2,1)}, bf16[512,1024]{1,0:T(8,128)(2,1)}) custom-call(bf16[512,128]{1,0:T(8,128)(2,1)S(1)} %get-tuple-element.9.back_ref, bf16[4,512,128]{2,1,0:T(8,128)(2,1)S(1)} %get-tuple-element.10.k_ref, bf16[4,512,256]{2,1,0:T(8,128)(2,1)S(1)} %get-tuple-element.11.v_ref, ...), custom_call_target="tpu_custom_call" | custom-call | flops 500000000 | bytes 8000000 | tf_op jit(solution)/shard_map/pallas_call | solution.py:511

commit v6 on v5

--- a/solution.py
+++ b/solution.py
@@ -23,7 +23,7 @@
 F32 = jnp.float32
 BF16 = jnp.bfloat16
 
-S0, S1, S2, S4, R0, R1, R2, R3, N_SEM = 0, 1, 8, 11, 16, 27, 67, 70, 86
+S0, S1, S2, S4, R0, R1, R2, R3, N_SEM = 0, 1, 8, 11, 16, 27, 32, 35, 36
 FAR_FIRST = (4, 5, 3, 7, 6, 2, 1)
 
 
@@ -49,7 +49,7 @@
     qp, w4, gath, dout, kT, qT, lam, inner, sm,
     gsb, pgs, zbuf, xbuf, state_low,
     lg, rb0, rbh, rsrc, rbuf, tsrc, tbuf, rets, rfin,
-    pacc, lgacc, codes_ref, table_ref,
+    pacc, lgacc, rest, codes_ref, table_ref,
     loc_sem, ys, yr, ss, sr,
 ):
     g = lax.axis_index("seq")
@@ -250,22 +250,27 @@
         for n in range(PAIRS):
             project_pair(n, *how)
 
-    def level_part(p, e, first, count):
-        h = 2 * p + e
-        rows = qT[p, e * 64:(e + 1) * 64, first:first + count].astype(F32)
+    def scaled_queries(p, e, first):
+        rows = qT[p, e * 64:(e + 1) * 64, first:first + HALF].astype(F32)
         scaled = [
-            (lam[LB + 1 + b, pl.ds(h, 1), :][:, first:first + count] * rows).astype(BF16) for b in range(SEQ_BITS)
+            (lam[LB + 1 + b, pl.ds(2 * p + e, 1), :][:, first:first + HALF] * rows).astype(BF16)
+            for b in range(SEQ_BITS)
         ]
-        return nn(jnp.concatenate(scaled, axis=0), dout[h, first:first + count, :])
+        return jnp.concatenate(scaled, axis=0)
 
     def level_first(p, _):
         for e in range(2):
-            lgacc[p, e] = level_part(p, e, 0, HALF)
+            lgacc[p, e] = nn(scaled_queries(p, e, 0), dout[2 * p + e, 0:HALF, :])
+        return 0
+
+    def scale_rest(p, _):
+        for e in range(2):
+            rest[p, e] = scaled_queries(p, e, HALF)
         return 0
 
     def level_last(p):
         for e in range(2):
-            grads = (lgacc[p, e] + level_part(p, e, HALF, HALF)).astype(BF16)
+            grads = (lgacc[p, e] + nn(rest[p, e], dout[2 * p + e, HALF:ROWS, :])).astype(BF16)
             at = pl.ds(pl.multiple_of(p * 128 + e * 64, 64), 64)
             for b in range(SEQ_BITS):
                 lg[b, at, :] = grads[b * 64:(b + 1) * 64, :]
@@ -298,6 +303,7 @@
     arrive(s2)
     s2 = start([remote(xbuf.at[1], xbuf.at[2], ss, sr, S2 + 1, x_peer(3))])
     project([left, right], HALF, HALF, False, False)
+    lax.fori_loop(0, PAIRS, scale_rest, 0)
     arrive(forwards[0])
     arrive(forwards[1])
     project([across], 0, HALF, False, True)
@@ -308,35 +314,49 @@
     arrive(forwards[3])
     project([across], HALF + CROWS, CROWS, False, True)
 
-    r0 = []
+    r0 = [[], []]
     for i in range(2):
         p = 2 * (1 - c) + i
         level_last(p)
         rows = pl.ds(pl.multiple_of(p * 128, 128), 128)
-        r0 += start([
-            remote(lg.at[1 + b, rows], rbh.at[b, pl.ds(i * 128, 128)], ss, sr, R0 + 5 * i + b, partner)
-            for b in range(5)
-        ])
+        for b in (3, 4, 0, 1, 2):
+            r0[b // 3] += start([
+                remote(lg.at[1 + b, rows], rbh.at[b, pl.ds(i * 128, 128)], ss, sr, R0 + 5 * i + b, partner)
+            ])
     for i in range(2):
         level_last(2 * c + i)
-    arrive(r0)
-    rsrc[...] = (lg[pl.ds(1, 5), mine, :].astype(F32) + rbh[...].astype(F32)).astype(BF16)
 
     def owned(at):
         return pl.ds(pl.multiple_of(at * SLICE, SLICE), SLICE)
 
+    def chip_sum(first, count):
+        levels = pl.ds(first, count)
+        rsrc[levels] = (lg[pl.ds(1 + first, count), mine, :].astype(F32) + rbh[levels].astype(F32)).astype(BF16)
+
     def slice_of(i, level):
-        return remote(
-            rsrc.at[level, owned(flipped(z, i, 3))], rbuf.at[i, level], ss, sr, R1 + 8 * level + i, z_peer(i)
-        )
-
-    upper = [x % 2 == 1, x // 2 == 1]
+        return remote(rsrc.at[level, owned(flipped(z, i, 3))], rbuf.at[i, level], ss, sr, R1 + level, z_peer(i))
+
+    def slices(count, level):
+        some = rbuf.at[pl.ds(1, count), level]
+        return remote(some, some, ss, sr, R1 + level, z_peer(1))
+
+    set_bits = [(z // 2**b) % 2 for b in range(3)] + [x % 2, x // 2]
+
+    def send_level(i, level):
+        @pl.when(set_bits[level] == 1)
+        def _():
+            slice_of(i, level).start()
+
+    arrive(r0[1])
+    chip_sum(3, 2)
     for i in FAR_FIRST:
-        for b in range(2):
-            start_if(upper[b], [slice_of(i, 3 + b)])
+        for level in (3, 4):
+            send_level(i, level)
+    arrive(r0[0])
+    chip_sum(0, 3)
     for i in FAR_FIRST:
-        for b in range(3):
-            start_if((z // 2**b) % 2 == 1, [slice_of(i, b)])
+        for level in range(3):
+            send_level(i, level)
     rbuf[0] = rsrc[:, owned(z), :]
     rb = start([remote(lg.at[0], rb0, ss, sr, R0 + 10, partner)])
     arrive(s2)
@@ -384,45 +404,61 @@
         return 0
 
     lax.fori_loop(0, 2, attention, 0)
-    for b in range(2):
-        arrive_if(upper[b], [slice_of(i, 3 + b) for i in FAR_FIRST])
+    for copy in sent:
+        copy.wait_send()
+    sent.clear()
+    for level in (3, 4):
+        @pl.when(set_bits[level] == 1)
+        def _(level=level):
+            slices(7, level).wait_recv()
     tops = rbuf[0, pl.ds(3, 2)].astype(F32)
     for i in range(1, 8):
         tops = tops + rbuf[i, pl.ds(3, 2)].astype(F32)
     tsrc[...] = tops.astype(BF16)
     near = [remote(tsrc.at[0], tbuf.at[1, 0], ss, sr, R2, x_peer(1))]
     far = [remote(tsrc.at[1], tbuf.at[i, 1], ss, sr, R2 + i - 1, x_peer(i)) for i in (2, 3)]
-    start_if(upper[1], far)
-    start_if(upper[0], near)
+    start_if(x // 2 == 1, far)
+    start_if(x % 2 == 1, near)
 
     lax.fori_loop(2, 4, attention, 0)
-    for i in FAR_FIRST:
-        for b in range(3):
-            arrive_if((flipped(z, i, 3) // 2**b) % 2 == 1, [slice_of(i, b)])
+    for level in range(3):
+        @pl.when(set_bits[level] == 1)
+        def _(level=level):
+            slices(3, level).wait_recv()
+
+        @pl.when(set_bits[level] == 0)
+        def _(level=level):
+            slices(4, level).wait_recv()
     arrive_if(x % 2 == 0, near)
     arrive_if(x // 2 == 0, far)
     outer = tbuf[1, 0].astype(F32) + tbuf[2, 1].astype(F32) + tbuf[3, 1].astype(F32)
     finals = pl.ds(pl.multiple_of(c * HALF + z * SLICE, SLICE), SLICE)
-    r3 = []
     for r in FAR_FIRST + (0,):
         total = outer
         for i in range(1, 8):
             total = total + rbuf[r ^ i, i.bit_length() - 1].astype(F32)
         rets[r] = total.astype(BF16)
         if r:
-            r3 += start([remote(rets.at[r], rfin.at[finals], ss, sr, R3 + r, z_peer(r))])
-        r3 += start([remote(rets.at[r], rfin.at[finals], ss, sr, R3 + 8 + r, z_other(r) if r else partner)])
+            remote(rets.at[r], rfin.at[finals], ss, sr, R3, z_peer(r)).start()
+        remote(rets.at[r], rfin.at[finals], ss, sr, R3, z_other(r) if r else partner).start()
     rfin[finals, :] = rets[0]
-    arrive(rb)
-    arrive(r3)
-    ret_ref[...] = (rfin[...].astype(F32) + rb0[...].astype(F32)).astype(BF16)
     for copy in sent:
         copy.wait_send()
+    for level in range(5):
+        @pl.when(set_bits[level] == 1)
+        def _(level=level):
+            slices(7, level).wait_send()
     for condition, copies in sent_if:
         @pl.when(condition)
         def _(copies=copies):
             for copy in copies:
                 copy.wait_send()
+    arrive(rb)
+    every = rfin.at[pl.ds(0, 15 * SLICE)]
+    last = remote(every, every, ss, sr, R3, partner)
+    last.wait_recv()
+    ret_ref[...] = (rfin[...].astype(F32) + rb0[...].astype(F32)).astype(BF16)
+    last.wait_send()
 
 
 def finish(back_ref, k_ref, v_ref, q_ref, kacc_ref, vacc_ref, qo_hbm, ko_hbm, vo_hbm, ko, vo, sem):
@@ -478,6 +514,7 @@
         pltpu.VMEM((ROWS, 128), BF16),
         pltpu.VMEM((4, ROWS, 256), F32),
         pltpu.VMEM((PAIRS, 2, SEQ_BITS * 64, 128), F32),
+        pltpu.VMEM((PAIRS, 2, SEQ_BITS * 64, HALF), BF16),
         pltpu.VMEM((12, HEADS, ROWS), jnp.int32),
         pltpu.VMEM((HEADS, 16), F32),
         pltpu.SemaphoreType.DMA((19,)),

time: 57.3 us -> 55.7 us (0.972)
  Pallas kernels: 56.5 us -> 55 us
    pallas_call x1, Pallas kernels: 55 us -> 53.4 us  [per_device(): pl.pallas_call(kernel, out_shape=(pltpu.VMEM((PAIRS, ROWS, 128), BF16), p...]
where the time goes in v6:
time: 55.7 us; the launch traced here: 55.6 us
  Pallas kernels  55 us (99%)
  between operations  0.64 us (1%)
    pallas_call x1, Pallas kernels, per_device(): pl.pallas_call(kernel, out_shape=(pltpu.VMEM((PAIRS, ROWS, 128), BF16), p...  53.4 us
    pallas_call x1, Pallas kernels, per_device(): pl.pallas_call(finish, out_shape=(jax.ShapeDtypeStruct((ROWS, HEADS * DK)...  1.54 us

profile of v6, /device:TPU:1, one launch (start us, length us, event | category | flops | bytes accessed | tf_op | source)
XLA Modules:
  0.0 55.6 jit_solution(13492061431881456343)
XLA Ops:
  0.6 53.4 %shard_map.94 = (bf16[4,512,128]{2,1,0:T(8,128)(2,1)S(1)}, f32[4,512,128]{2,1,0:T(8,128)S(1)}, f32[4,512,256]{2,1,0:T(8,128)S(1)}, bf16[512,128]{1,0:T(8,128)(2,...) custom-call(bf16[512,512]{1,0:T(8,128)(2,1)} %q_hbm.1, bf16[512,512]{1,0:T(8,128)(2,1)} %k_hbm.1, ...), custom_call_target="tpu_custom_call" | custom-call | flops 8000000000 | bytes 12000000 | tf_op jit(solution)/shard_map/pallas_call | solution.py:530
  54.1 1.5 %shard_map.95 = (bf16[512,512]{1,0:T(8,128)(2,1)}, bf16[512,512]{1,0:T(8,128)(2,1)}, bf16[512,1024]{1,0:T(8,128)(2,1)}) custom-call(bf16[512,128]{1,0:T(8,128)(2,1)S(1)} %get-tuple-element.9.back_ref, bf16[4,512,128]{2,1,0:T(8,128)(2,1)S(1)} %get-tuple-element.10.k_ref, bf16[4,512,256]{2,1,0:T(8,128)(2,1)S(1)} %get-tuple-element.11.v_ref, ...), custom_call_target="tpu_custom_call" | custom-call | flops 500000000 | bytes 8000000 | tf_op jit(solution)/shard_map/pallas_call | solution.py:548

commit v7 on v6

--- a/solution.py
+++ b/solution.py
@@ -49,7 +49,7 @@
     qp, w4, gath, dout, kT, qT, lam, inner, sm,
     gsb, pgs, zbuf, xbuf, state_low,
     lg, rb0, rbh, rsrc, rbuf, tsrc, tbuf, rets, rfin,
-    pacc, lgacc, rest, codes_ref, table_ref,
+    pacc, lgacc, rest, qacc, w_turned, codes_ref, table_ref,
     loc_sem, ys, yr, ss, sr,
 ):
     g = lax.axis_index("seq")
@@ -237,7 +237,10 @@
         rows = pl.ds(first, count)
         total = None if begin else pacc[n, rows, :]
         for d in slots:
-            part = nt(gath[d, rows, :], w4[d, cols, :])
+            if end:
+                part = nn(gath[d, rows, :], w_turned[:, cols])
+            else:
+                part = nt(gath[d, rows, :], w4[d, cols, :])
             total = part if total is None else total + part
         if end:
             low = total.astype(BF16)
@@ -289,6 +292,7 @@
     start(s1[3])
     turn(2)
 
+    turn(3)
     arrive(s1[3])
     parts = [zbuf[flipped(z, i, 3)].astype(F32) for i in range(8)]
     pair1 = parts[2] + parts[3]
@@ -299,11 +303,12 @@
     state_low[2, mine, :] = pair1.astype(BF16)
     state_low[3, mine, :] = quad.astype(BF16)
 
-    turn(3)
     arrive(s2)
     s2 = start([remote(xbuf.at[1], xbuf.at[2], ss, sr, S2 + 1, x_peer(3))])
     project([left, right], HALF, HALF, False, False)
     lax.fori_loop(0, PAIRS, scale_rest, 0)
+    for n in range(PAIRS):
+        w_turned[:, n * 256:(n + 1) * 256] = w4[across, n * 256:(n + 1) * 256, :].T
     arrive(forwards[0])
     arrive(forwards[1])
     project([across], 0, HALF, False, True)
@@ -315,14 +320,19 @@
     project([across], HALF + CROWS, CROWS, False, True)
 
     r0 = [[], []]
+
+    def swap(i, levels):
+        rows = pl.ds(pl.multiple_of((2 * (1 - c) + i) * 128, 128), 128)
+        return start([
+            remote(lg.at[1 + b, rows], rbh.at[b, pl.ds(i * 128, 128)], ss, sr, R0 + 5 * i + b, partner)
+            for b in levels
+        ])
+
     for i in range(2):
-        p = 2 * (1 - c) + i
-        level_last(p)
-        rows = pl.ds(pl.multiple_of(p * 128, 128), 128)
-        for b in (3, 4, 0, 1, 2):
-            r0[b // 3] += start([
-                remote(lg.at[1 + b, rows], rbh.at[b, pl.ds(i * 128, 128)], ss, sr, R0 + 5 * i + b, partner)
-            ])
+        level_last(2 * (1 - c) + i)
+        r0[1] += swap(i, (4, 3))
+    for i in range(2):
+        r0[0] += swap(i, (0, 1, 2))
     for i in range(2):
         level_last(2 * c + i)
 
@@ -349,8 +359,8 @@
 
     arrive(r0[1])
     chip_sum(3, 2)
-    for i in FAR_FIRST:
-        for level in (3, 4):
+    for level in (4, 3):
+        for i in FAR_FIRST:
             send_level(i, level)
     arrive(r0[0])
     chip_sum(0, 3)
@@ -359,19 +369,10 @@
             send_level(i, level)
     rbuf[0] = rsrc[:, owned(z), :]
     rb = start([remote(lg.at[0], rb0, ss, sr, R0 + 10, partner)])
-    arrive(s2)
-    state_low[4, mine, :] = xbuf[1]
-    state_low[5, mine, :] = (xbuf[2].astype(F32) + xbuf[3].astype(F32)).astype(BF16)
-    s4 = start([
-        remote(state_low.at[b, mine], state_low.at[b, mine], ss, sr, S4 + b - 1, partner) for b in range(1, SEQ_BITS)
-    ])
-    arrive(s4)
-
     def attention(p, _):
         turned_k = kT[p]
         values = vp[p]
         query = qp[p]
-        lines = []
         for e in range(2):
             h = 2 * p + e
             mine_q = masked(query, e)
@@ -394,12 +395,19 @@
             own_k = turned_k[e * 64:(e + 1) * 64, :]
             line = nn(own_k[:, :HALF], low)
             line_high = nn(own_k[:, HALF:], high)
+            qacc[p, pl.ds(e * 64, 64), :] = jnp.concatenate([line[:, :HALF], line[:, HALF:] + line_high], axis=1)
+        return 0
+
+    def read_states(p, _):
+        lines = []
+        for e in range(2):
+            h = 2 * p + e
             at = pl.ds(pl.multiple_of(h * 64, 64), 64)
-            states = state_low[:, at, :].reshape(SEQ_BITS * 64, 128)
-            read = nt(states, d)
+            read = nt(state_low[:, at, :].reshape(SEQ_BITS * 64, 128), dout[h])
+            line = qacc[p, pl.ds(e * 64, 64), :]
             for b in range(SEQ_BITS):
                 line = line + lam[LB + 1 + b, pl.ds(h, 1), :] * read[b * 64:(b + 1) * 64, :]
-            lines.append(jnp.concatenate([line[:, :HALF], line[:, HALF:] + line_high], axis=1))
+            lines.append(line)
         qo[p] = jnp.concatenate(lines, axis=0).T.astype(BF16)
         return 0
 
@@ -407,19 +415,25 @@
     for copy in sent:
         copy.wait_send()
     sent.clear()
-    for level in (3, 4):
+    near = [remote(tsrc.at[0], tbuf.at[1, 0], ss, sr, R2, x_peer(1))]
+    far = [remote(tsrc.at[1], tbuf.at[i, 1], ss, sr, R2 + i - 1, x_peer(i)) for i in (2, 3)]
+    arrive(s2)
+    for level, copies in ((4, far), (3, near)):
         @pl.when(set_bits[level] == 1)
         def _(level=level):
             slices(7, level).wait_recv()
-    tops = rbuf[0, pl.ds(3, 2)].astype(F32)
-    for i in range(1, 8):
-        tops = tops + rbuf[i, pl.ds(3, 2)].astype(F32)
-    tsrc[...] = tops.astype(BF16)
-    near = [remote(tsrc.at[0], tbuf.at[1, 0], ss, sr, R2, x_peer(1))]
-    far = [remote(tsrc.at[1], tbuf.at[i, 1], ss, sr, R2 + i - 1, x_peer(i)) for i in (2, 3)]
-    start_if(x // 2 == 1, far)
-    start_if(x % 2 == 1, near)
-
+
+        top = rbuf[0, level].astype(F32)
+        for i in range(1, 8):
+            top = top + rbuf[i, level].astype(F32)
+        tsrc[level - 3] = top.astype(BF16)
+        start_if(set_bits[level] == 1, copies)
+
+    state_low[4, mine, :] = xbuf[1]
+    state_low[5, mine, :] = (xbuf[2].astype(F32) + xbuf[3].astype(F32)).astype(BF16)
+    s4 = start([
+        remote(state_low.at[b, mine], state_low.at[b, mine], ss, sr, S4 + b - 1, partner) for b in range(1, SEQ_BITS)
+    ])
     lax.fori_loop(2, 4, attention, 0)
     for level in range(3):
         @pl.when(set_bits[level] == 1)
@@ -442,6 +456,8 @@
             remote(rets.at[r], rfin.at[finals], ss, sr, R3, z_peer(r)).start()
         remote(rets.at[r], rfin.at[finals], ss, sr, R3, z_other(r) if r else partner).start()
     rfin[finals, :] = rets[0]
+    arrive(s4)
+    lax.fori_loop(0, PAIRS, read_states, 0)
     for copy in sent:
         copy.wait_send()
     for level in range(5):
@@ -515,6 +531,8 @@
         pltpu.VMEM((4, ROWS, 256), F32),
         pltpu.VMEM((PAIRS, 2, SEQ_BITS * 64, 128), F32),
         pltpu.VMEM((PAIRS, 2, SEQ_BITS * 64, HALF), BF16),
+        pltpu.VMEM((PAIRS, 128, ROWS), F32),
+        pltpu.VMEM((FEAT, HEADS * DV), BF16),
         pltpu.VMEM((12, HEADS, ROWS), jnp.int32),
         pltpu.VMEM((HEADS, 16), F32),
         pltpu.SemaphoreType.DMA((19,)),

time: 55.7 us -> 54.7 us (0.982)
  Pallas kernels: 55 us -> 54 us
    pallas_call x1, Pallas kernels: 53.4 us -> 52.4 us  [per_device(): pl.pallas_call(kernel, out_shape=(pltpu.VMEM((PAIRS, ROWS, 128), BF16), p...]
where the time goes in v7:
time: 54.7 us; the launch traced here: 54.6 us
  Pallas kernels  54 us (99%)
  between operations  0.64 us (1%)
    pallas_call x1, Pallas kernels, per_device(): pl.pallas_call(kernel, out_shape=(pltpu.VMEM((PAIRS, ROWS, 128), BF16), p...  52.4 us
    pallas_call x1, Pallas kernels, per_device(): pl.pallas_call(finish, out_shape=(jax.ShapeDtypeStruct((ROWS, HEADS * DK)...  1.54 us

profile of v7, /device:TPU:1, one launch (start us, length us, event | category | flops | bytes accessed | tf_op | source)
XLA Modules:
  0.0 54.6 jit_solution(13337257041074002588)
XLA Ops:
  0.6 52.4 %shard_map.94 = (bf16[4,512,128]{2,1,0:T(8,128)(2,1)S(1)}, f32[4,512,128]{2,1,0:T(8,128)S(1)}, f32[4,512,256]{2,1,0:T(8,128)S(1)}, bf16[512,128]{1,0:T(8,128)(2,...) custom-call(bf16[512,512]{1,0:T(8,128)(2,1)} %q_hbm.1, bf16[512,512]{1,0:T(8,128)(2,1)} %k_hbm.1, ...), custom_call_target="tpu_custom_call" | custom-call | flops 8000000000 | bytes 12000000 | tf_op jit(solution)/shard_map/pallas_call | solution.py:548
  53.1 1.5 %shard_map.95 = (bf16[512,512]{1,0:T(8,128)(2,1)}, bf16[512,512]{1,0:T(8,128)(2,1)}, bf16[512,1024]{1,0:T(8,128)(2,1)}) custom-call(bf16[512,128]{1,0:T(8,128)(2,1)S(1)} %get-tuple-element.9.back_ref, bf16[4,512,128]{2,1,0:T(8,128)(2,1)S(1)} %get-tuple-element.10.k_ref, bf16[4,512,256]{2,1,0:T(8,128)(2,1)S(1)} %get-tuple-element.11.v_ref, ...), custom_call_target="tpu_custom_call" | custom-call | flops 500000000 | bytes 8000000 | tf_op jit(solution)/shard_map/pallas_call | solution.py:566

commit v8 on v7

--- a/solution.py
+++ b/solution.py
@@ -357,9 +357,9 @@
         def _():
             slice_of(i, level).start()
 
-    arrive(r0[1])
-    chip_sum(3, 2)
-    for level in (4, 3):
+    for at, level in enumerate((4, 3)):
+        arrive(r0[1][at::2])
+        chip_sum(level, 1)
         for i in FAR_FIRST:
             send_level(i, level)
     arrive(r0[0])

time: 54.7 us -> 54.7 us (level)
  no operation moved by 1% of the time
where the time goes in v8:
time: 54.7 us; the launch traced here: 54.6 us
  Pallas kernels  54 us (99%)
  between operations  0.64 us (1%)
    pallas_call x1, Pallas kernels, per_device(): pl.pallas_call(kernel, out_shape=(pltpu.VMEM((PAIRS, ROWS, 128), BF16), p...  52.4 us
    pallas_call x1, Pallas kernels, per_device(): pl.pallas_call(finish, out_shape=(jax.ShapeDtypeStruct((ROWS, HEADS * DK)...  1.54 us

profile of v8, /device:TPU:1, one launch (start us, length us, event | category | flops | bytes accessed | tf_op | source)
XLA Modules:
  0.0 54.6 jit_solution(8975955958128677526)
XLA Ops:
  0.6 52.4 %shard_map.94 = (bf16[4,512,128]{2,1,0:T(8,128)(2,1)S(1)}, f32[4,512,128]{2,1,0:T(8,128)S(1)}, f32[4,512,256]{2,1,0:T(8,128)S(1)}, bf16[512,128]{1,0:T(8,128)(2,...) custom-call(bf16[512,512]{1,0:T(8,128)(2,1)} %q_hbm.1, bf16[512,512]{1,0:T(8,128)(2,1)} %k_hbm.1, ...), custom_call_target="tpu_custom_call" | custom-call | flops 8000000000 | bytes 12000000 | tf_op jit(solution)/shard_map/pallas_call | solution.py:548
  53.1 1.5 %shard_map.95 = (bf16[512,512]{1,0:T(8,128)(2,1)}, bf16[512,512]{1,0:T(8,128)(2,1)}, bf16[512,1024]{1,0:T(8,128)(2,1)}) custom-call(bf16[512,128]{1,0:T(8,128)(2,1)S(1)} %get-tuple-element.9.back_ref, bf16[4,512,128]{2,1,0:T(8,128)(2,1)S(1)} %get-tuple-element.10.k_ref, bf16[4,512,256]{2,1,0:T(8,128)(2,1)S(1)} %get-tuple-element.11.v_ref, ...), custom_call_target="tpu_custom_call" | custom-call | flops 500000000 | bytes 8000000 | tf_op jit(solution)/shard_map/pallas_call | solution.py:566
